TPU v7x, 256 devices: a whole 4x4x8 slice. The times are simulated.
256 devices in a mesh: rep: 64 (over z, y_lo, x), fsdp: 4 (over y_hi, core).
Axes of the slice: x: 4, y: 4 (y_hi: 2, y_lo: 2; y = y_hi * 2 + y_lo), z: 8, core: 2. Of those that a mesh axis runs over, the one named last changes fastest.
Arguments:
- tokens: bfloat16 [64, 1024, 4096], P('rep', 'fsdp'), as said below
- gain: float32 [64, 4096], P('rep'), may hold values from 0.1 to 1.9
- weight: bfloat16 [64, 1024, 4096], P('rep', 'fsdp'), may hold values from -6 to 6
- momentum: bfloat16 [64, 1024, 4096], P('rep', 'fsdp'), may hold values from -6 to 6
- key_grad: bfloat16 [64, 1024, 1024], P('rep', 'fsdp'), may hold values from -6 to 6
- step: int32 [1], replicated, may hold values from 0 to 999
Outputs:
- projected: bfloat16 [64, 1024, 1024], P('rep', 'fsdp')
- weight_out: bfloat16 [64, 1024, 4096], P('rep', 'fsdp')
- momentum_out: bfloat16 [64, 1024, 4096], P('rep', 'fsdp')
Inputs may be any that keep to these rules, and one draw needn't show every extreme that they name: `tokens`: activations entering the layer.
All inputs are finite; a program needn't handle non-finite values.
Results may differ from a plain program's by a relative error of at most 0.0055.
Values may be sent and summed in bfloat16 or wider, within the bound.
No kernel may reach another device: no remote copies, remote signals or barrier semaphores. Data moves between devices by JAX's collectives and lax.ppermute only.
A program may use at most 128 MiB of HBM per device.

v0:
```python
from functools import partial

import jax
import jax.numpy as jnp
from jax import lax
from jax.experimental import pallas as pl
from jax.experimental.pallas import tpu as pltpu
from jax.sharding import PartitionSpec as P

epsilon = 1e-05
moment_decay = 0.9
AXES = ("rep", "fsdp")
PARTS = 2


def norm_kernel(place, tok, gains, k_far, k_cross, *parts):
    rows, model = tok.shape
    width = model // len(parts)
    block = k_far.shape[1]
    step, piece = 16, 512

    @pl.loop(0, rows // step)
    def _(i):
        at = pl.ds(pl.multiple_of(i * step, step), step)
        squares = jnp.zeros((step, piece), jnp.float32)
        for c in range(0, model, piece):
            values = tok[at, c : c + piece].astype(jnp.float32)
            squares += values * values
        inverse = lax.rsqrt(jnp.sum(squares, axis=-1, keepdims=True) / model + epsilon)
        for c in range(0, model, piece):
            values = tok[at, c : c + piece].astype(jnp.float32)
            normed = (values * inverse * gains[:, c : c + piece]).astype(jnp.bfloat16)
            parts[c // width][at, c % width : c % width + piece] = normed

    parts[0][:, width : width + block] = k_far[...]
    parts[0][:, width + block :] = k_cross[...]


def normalize(tok, gains, grads, place):
    rows, model = tok.shape
    block = grads.shape[1] // 4
    step = 64
    widths = [model // PARTS + (2 * block if i == 0 else 0) for i in range(PARTS)]

    def k_spec(flip):
        return pl.BlockSpec((step, block), lambda i, p: (i, p[0] ^ flip))

    return pl.pallas_call(
        norm_kernel,
        grid_spec=pltpu.PrefetchScalarGridSpec(
            num_scalar_prefetch=1,
            grid=(rows // step,),
            in_specs=[
                pl.BlockSpec((step, model), lambda i, p: (i, 0)),
                pl.BlockSpec((1, model), lambda i, p: (0, 0)),
                k_spec(2),
                k_spec(3),
            ],
            out_specs=[pl.BlockSpec((step, w), lambda i, p: (i, 0)) for w in widths],
        ),
        out_shape=[jax.ShapeDtypeStruct((rows, w), jnp.bfloat16) for w in widths],
        cost_estimate=pl.CostEstimate(
            flops=4 * rows * model, bytes_accessed=5 * rows * model, transcendentals=rows
        ),
        name="normalize",
    )(place, tok, gains, grads, grads)


def pack_kernel(place, *refs):
    *parts, weights, grads, whole, held, sems = refs
    width, model = weights.shape[1] // len(parts), weights.shape[1]
    block = grads.shape[1] // 4
    keys = pl.ds(pl.multiple_of((place[0] ^ 1) * block, block), block)
    pieces = [(part.at[:, :width], p * width, width) for p, part in enumerate(parts)]
    pieces += [(weights, model, model), (grads.at[:, keys], 2 * model, block)]
    copies = [
        pltpu.make_async_copy(ref, held.at[:, at : at + size], sems.at[i])
        for i, (ref, at, size) in enumerate(pieces)
    ]
    for copy in copies:
        copy.start()
    for copy in copies:
        copy.wait()
    out = pltpu.make_async_copy(held, whole, sems.at[len(copies)])
    out.start()
    out.wait()


def pack(parts, weights, grads, place):
    rows, model = weights.shape
    shape = (rows, 2 * model + grads.shape[1] // 4)
    hbm = pl.BlockSpec(memory_space=pltpu.HBM)
    return pl.pallas_call(
        pack_kernel,
        in_specs=[pl.BlockSpec(memory_space=pltpu.SMEM)] + [hbm] * (len(parts) + 2),
        out_specs=hbm,
        out_shape=jax.ShapeDtypeStruct(shape, jnp.bfloat16),
        scratch_shapes=[pltpu.VMEM(shape, jnp.bfloat16), pltpu.SemaphoreType.DMA((len(parts) + 3,))],
        compiler_params=pltpu.CompilerParams(vmem_limit_bytes=16 << 20),
        cost_estimate=pl.CostEstimate(flops=0, bytes_accessed=4 * shape[0] * shape[1], transcendentals=0),
        name="pack",
    )(place, *parts, weights, grads)


def moment_kernel(scale, piece, place, k_own, k_sib, k_far, k_cross, n_own, n_sib, n_far, n_cross, moments, new, sent, keys, turned):
    @pl.when(pl.program_id(0) == 0)
    def _():
        @pl.loop(0, k_own.shape[0] // 32)
        def _(i):
            at = pl.ds(pl.multiple_of(i * 32, 32), 32)
            for s, k in enumerate((k_own, k_sib, k_far, k_cross)):
                keys[s, at, :] = k[at, :]

        @pl.loop(0, 4)
        def _(s):
            turned[s] = keys[s].T

    @pl.loop(0, new.shape[1] // piece)
    def _(i):
        at = pl.ds(pl.multiple_of(i * piece, piece), piece)
        total = None
        for s, n in enumerate((n_own, n_sib, n_far, n_cross)):
            product = jnp.dot(turned[s], n[:, at], preferred_element_type=jnp.float32)
            total = product if total is None else total + product
        value = moment_decay * moments[:, at].astype(jnp.float32) + total * scale
        new[:, at] = value
        sent[:, at] = value.astype(jnp.bfloat16)


def moment_part(scale, place, grads, own, sib, far, cross, first, moments, start, columns):
    rows, model = moments.shape
    tokens = own.shape[0]
    tile = 512
    k_specs = [
        pl.BlockSpec((tokens, rows), lambda i, p: (0, p[0])),
        pl.BlockSpec((tokens, rows), lambda i, p: (0, 2 * model // rows)),
        pl.BlockSpec((tokens, rows), lambda i, p: (0, columns // rows)),
        pl.BlockSpec((tokens, rows), lambda i, p: (0, columns // rows + 1)),
    ]
    whole_spec = pl.BlockSpec((tokens, tile), lambda i, p: (0, start // tile + i))
    part_spec = pl.BlockSpec((tokens, tile), lambda i, p: (0, i))
    m_spec = pl.BlockSpec((rows, tile), lambda i, p: (0, start // tile + i))
    o_spec = pl.BlockSpec((rows, tile), lambda i, p: (0, i))
    return pl.pallas_call(
        partial(moment_kernel, scale, 256),
        grid_spec=pltpu.PrefetchScalarGridSpec(
            num_scalar_prefetch=1,
            grid=(columns // tile,),
            in_specs=k_specs + [whole_spec] * 2 + [part_spec] * 2 + [m_spec],
            out_specs=[o_spec, o_spec],
            scratch_shapes=[
                pltpu.VMEM((4, tokens, rows), jnp.bfloat16),
                pltpu.VMEM((4, rows, tokens), jnp.bfloat16),
            ],
        ),
        out_shape=[
            jax.ShapeDtypeStruct((rows, columns), jnp.float32),
            jax.ShapeDtypeStruct((rows, columns), jnp.bfloat16),
        ],
        cost_estimate=pl.CostEstimate(
            flops=8 * tokens * rows * columns,
            bytes_accessed=(8 * tokens + 8 * rows) * columns,
            transcendentals=0,
        ),
        name="moment_part",
    )(place, grads, sib, *first, own, sib, far, cross, moments)


def project_kernel(scale, per, *refs):
    *sources, own, other, out, total = refs
    i = pl.program_id(0)
    rows = own.shape[0]

    piece, step = 256, 32

    @pl.when(i == 0)
    def _():
        @pl.loop(0, total.shape[0] // step)
        def _(r):
            at = pl.ds(pl.multiple_of(r * step, step), step)
            total[at, :] = jnp.zeros((step, total.shape[1]), jnp.float32)

    for part, source in enumerate(sources):

        @pl.when(i // per == part)
        def _(source=source):
            @pl.loop(0, own.shape[1] // piece)
            def _(c):
                at = pl.ds(pl.multiple_of(c * piece, piece), piece)
                for g, weights in enumerate((own, other)):
                    total[:, g * rows : (g + 1) * rows] += lax.dot_general(
                        source[:, at],
                        weights[:, at],
                        (((1,), (1,)), ((), ())),
                        preferred_element_type=jnp.float32,
                    )

    @pl.when(i == pl.num_programs(0) - 1)
    def _():
        @pl.loop(0, total.shape[0] // step)
        def _(r):
            at = pl.ds(pl.multiple_of(r * step, step), step)
            out[at, :] = (total[at, :] * scale).astype(jnp.bfloat16)


def project(scale, parts, own, other, offset):
    tokens = parts[0].shape[0]
    rows, model = own.shape
    tile = 512
    tiles = model // tile
    per = tiles // len(parts)
    n_specs = [
        pl.BlockSpec((tokens, tile), lambda i, part=part: (0, jnp.clip(i - part * per, 0, per - 1)))
        for part in range(len(parts))
    ]
    return pl.pallas_call(
        partial(project_kernel, scale, per),
        grid=(tiles,),
        in_specs=n_specs
        + [pl.BlockSpec((rows, tile), lambda i, at=at: (0, at // tile + i)) for at in (0, offset)],
        out_specs=pl.BlockSpec((tokens, 2 * rows), lambda i: (0, 0)),
        out_shape=jax.ShapeDtypeStruct((tokens, 2 * rows), jnp.bfloat16),
        scratch_shapes=[pltpu.VMEM((tokens, 2 * rows), jnp.float32)],
        cost_estimate=pl.CostEstimate(
            flops=4 * tokens * rows * model,
            bytes_accessed=(2 * tokens + 4 * rows) * model,
            transcendentals=0,
        ),
        name="project",
    )(*parts, own, other)


def place_kernel(place, *refs):
    *blocks, out = refs
    for k, block in enumerate(blocks):

        @pl.when(pl.program_id(0) == k)
        def _(block=block):
            @pl.loop(0, block.shape[0] // 32)
            def _(i):
                at = pl.ds(pl.multiple_of(i * 32, 32), 32)
                out[at, :] = block[at, :]


def place_blocks(place, blocks):
    rows, columns = blocks[0][0].shape
    width = columns // 2
    count = len(blocks)
    return pl.pallas_call(
        place_kernel,
        grid_spec=pltpu.PrefetchScalarGridSpec(
            num_scalar_prefetch=1,
            grid=(count,),
            in_specs=[pl.BlockSpec((rows, width), lambda i, p, half=half: (0, half)) for _, half in blocks],
            out_specs=pl.BlockSpec((rows, width), lambda i, p: (0, p[0] ^ i)),
        ),
        out_shape=jax.ShapeDtypeStruct((rows, count * width), jnp.bfloat16),
        cost_estimate=pl.CostEstimate(
            flops=0, bytes_accessed=4 * count * rows * width, transcendentals=0
        ),
        name="place_blocks",
    )(place, *[block for block, _ in blocks])


def average_kernel(start, rate, new, peer, weights, peer_weights, *refs):
    weight_out, moment_out, n_buf, p_buf, w_buf, q_buf, wo_buf, mo_buf, in_sems, out_sems = refs[-10:]
    tiles, rows, tile = n_buf.shape
    step = 32

    def columns(t, start):
        return pl.ds(pl.multiple_of(start + t * tile, tile), tile)

    def takes(t):
        pairs = ((new, 0, n_buf), (peer, 0, p_buf), (weights, start, w_buf), (peer_weights, start, q_buf))
        return [
            pltpu.make_async_copy(ref.at[:, columns(t, at)], buf.at[t], in_sems.at[t, i])
            for i, (ref, at, buf) in enumerate(pairs)
        ]

    def gives(t):
        return [
            pltpu.make_async_copy(buf.at[t], ref.at[:, columns(t, start)], out_sems.at[t, i])
            for i, (buf, ref) in enumerate(((wo_buf, weight_out), (mo_buf, moment_out)))
        ]

    @pl.loop(0, tiles)
    def _(t):
        for copy in takes(t):
            copy.start()

    @pl.loop(0, tiles)
    def _(t):
        for copy in takes(t):
            copy.wait()

        @pl.loop(0, rows // step)
        def _(i):
            at = pl.ds(pl.multiple_of(i * step, step), step)
            moment = (n_buf[t, at, :] + p_buf[t, at, :].astype(jnp.float32)) * 0.5
            weight = w_buf[t, at, :].astype(jnp.float32) + q_buf[t, at, :].astype(jnp.float32)
            wo_buf[t, at, :] = (weight * 0.5 - rate[0] * moment).astype(jnp.bfloat16)
            mo_buf[t, at, :] = moment.astype(jnp.bfloat16)

        for copy in gives(t):
            copy.start()

    @pl.loop(0, tiles)
    def _(t):
        for copy in gives(t):
            copy.wait()


def average_part(rate, new, peer, weights, peer_weights, start, outs):
    rows, model = weights.shape
    columns = new.shape[1]
    tile = 256
    tiles = columns // tile
    hbm = pl.BlockSpec(memory_space=pltpu.HBM)
    shape = jax.ShapeDtypeStruct((rows, model), jnp.bfloat16)
    buf = pltpu.VMEM((tiles, rows, tile), jnp.bfloat16)
    return pl.pallas_call(
        partial(average_kernel, start),
        in_specs=[pl.BlockSpec(memory_space=pltpu.SMEM)] + [hbm] * (4 + len(outs)),
        out_specs=[hbm, hbm],
        out_shape=[shape, shape],
        input_output_aliases={5 + i: i for i in range(len(outs))},
        scratch_shapes=[
            pltpu.VMEM((tiles, rows, tile), jnp.float32),
            *[buf] * 5,
            pltpu.SemaphoreType.DMA((tiles, 4)),
            pltpu.SemaphoreType.DMA((tiles, 2)),
        ],
        compiler_params=pltpu.CompilerParams(vmem_limit_bytes=24 << 20),
        cost_estimate=pl.CostEstimate(
            flops=6 * rows * columns, bytes_accessed=14 * rows * columns, transcendentals=0
        ),
        name="average_part",
    )(rate, new, peer, weights, peer_weights, *outs)


def stage(always, work, *operands):
    def idle(*operands):
        outs, tree = jax.tree.flatten(jax.eval_shape(work, *operands))
        blank = pl.pallas_call(
            lambda *refs: None,
            out_specs=[pl.BlockSpec(memory_space=pltpu.HBM)] * len(outs),
            out_shape=[jax.ShapeDtypeStruct(out.shape, out.dtype) for out in outs],
            name="blank",
        )()
        return jax.tree.unflatten(tree, blank)

    return lax.cond(always, work, idle, *operands)


def branch(bit, reps, shards, tok, gains, weights, moments, grads, place, rate, always):
    model = tok.shape[1]
    scale = float(model) ** (-0.5)
    rows = weights.shape[0]
    columns = model // PARTS
    low_bit = 2

    def move(value, rep_flip, shard_flip):
        pairs = [
            (r * shards + s, (r ^ rep_flip) * shards + (s ^ shard_flip))
            for r in range(reps)
            for s in range(shards)
        ]
        return lax.ppermute(value, AXES, pairs)

    flip = 1 << bit
    far_flip = flip if bit == low_bit else 0

    peer_weights = move(weights, flip, 0)
    own_parts = normalize(tok, gains, grads, place)
    far = [move(part, far_flip, 2) for part in own_parts]

    def near_stage(parts, weights, grads):
        own = pack(parts, weights, grads, place)
        sib = move(own, 0, 1)
        return own, sib, project(scale, [own], weights, sib, model)

    own, sib, near = stage(always, near_stage, own_parts, weights, grads)
    far[0], near = lax.optimization_barrier((far[0], near))

    def moment_stage(part, own, sib, here, first, grads, moments, share):
        there = move(here, 0, 1)
        shared = [move(value, 0, 1) for value in share]
        first = (here, there) if first is None else first
        new, sent = moment_part(
            scale, place, grads, own, sib, here, there, first, moments, part * columns, columns
        )
        return new, sent, there, shared

    new, peer, cross, sent, shared = [], [], [], None, []
    for part in range(PARTS):
        if part:
            far[part], sent = lax.optimization_barrier((far[part], sent))
        first = (far[0], cross[0]) if part else None
        share = [peer_weights] if part and far_flip else []
        value, sent, there, shared = stage(
            always, partial(moment_stage, part), own, sib, far[part], first, grads, moments, share
        )
        new.append(value)
        cross.append(there)
        if part == 0:
            sent, peer_weights = lax.optimization_barrier((sent, peer_weights))
        peer.append(move(sent, flip, 0))

    def average(part, outs):
        return average_part(rate, new[part], peer[part], weights, peer_weights, part * columns, outs)

    far[0], _ = lax.optimization_barrier((far[0], sent))
    if far_flip:
        distant = project(scale, far, peer_weights, shared[0], 0)
    else:
        distant = project(scale, far, weights, sib, model)
    distant, peer[0] = lax.optimization_barrier((distant, peer[0]))
    over = move(distant, far_flip, 2)
    over, outs = lax.optimization_barrier((over, average(0, ())))
    projected = place_blocks(place, ((near, 0), (near, 1), (over, 0), (over, 1)))
    peer[1], projected = lax.optimization_barrier((peer[1], projected))
    return (projected, *average(1, outs))


def local(tokens, gain, weight, momentum, key_grad, step):
    rate = 0.05 + 0.1 * step.astype(jnp.float32) / 1000.0
    reps, shards = lax.axis_size("rep"), lax.axis_size("fsdp")
    levels = min(5, reps.bit_length() - 1)
    place = lax.axis_index("fsdp").reshape(1)
    branches = [partial(branch, bit, reps, shards) for bit in range(levels)]
    outs = lax.switch(
        step[0] % levels,
        branches,
        tokens[0],
        gain,
        weight[0],
        momentum[0],
        key_grad[0],
        place,
        rate,
        step[0] >= 0,
    )
    return tuple(out[None] for out in outs)


def solution(mesh):
    split = P("rep", "fsdp", None)
    return jax.shard_map(
        local,
        mesh=mesh,
        in_specs=(split, P("rep", None), split, split, split, P()),
        out_specs=(split, split, split),
        check_vma=False,
    )
```

profile of v0, /device:TPU:1, one launch (start us, length us, event | category | flops | bytes accessed | tf_op | source)
XLA Modules:
  0.0 105.9 jit_solution(10696596793023346051)
XLA Ops:
  1.3 104.4 %conditional.16 = (bf16[256,1024]{1,0:T(8,128)(2,1)}, bf16[256,4096]{1,0:T(8,128)(2,1)}, bf16[256,4096]{1,0:T(8,128)(2,1)}) conditional(s32[]{:T(128)} %clamp.3, (pred[]{:T(512)}, s32[1]{0:T(128)}, bf16[256,4096]{1,0:T(8,128)(2,1)}, f32[1,4096]{1,0:T(1,128)}, bf16[256,1024]{1,0:T(8,128)(2,1)}, ...), branch_computations={%region_0.7_spmd, %region_7.14_spmd, %region_14.21_spmd, %region_2... | conditional | flops 4305453056 | bytes 154403648 | solution.py:431
  1.3 3.7 %collective-permute-start.14 = (bf16[256,4096]{1,0:T(8,128)(2,1)}, bf16[256,4096]{1,0:T(8,128)(2,1)S(1)}, u32[]{:S(2)}, u32[]{:S(2)}) collective-permute-start(bf16[256,4096]{1,0:T(8,128)(2,1)} %get-tuple-element.360.refs_2_.weights), channel_id=1, source_target_pairs={{0,8},{1,9},{2,10},{3,11},{4,12},{5,13},{6,14},{7,15},{8,0},{9,1},... | collective-permute-start | bytes 6291464 | tf_op jit(solution)/shard_map/cond/branch_1_fun/ppermute | solution.py:368
  5.0 4.8 %normalize.6 = (bf16[256,2560]{1,0:T(8,128)(2,1)}, bf16[256,2048]{1,0:T(8,128)(2,1)}) custom-call(s32[1]{0:T(128)} %get-tuple-element.354.place, bf16[256,4096]{1,0:T(8,128)(2,1)} %get-tuple-element.355.tok, f32[1,4096]{1,0:T(1,128)} %get-tuple-element.356.gains, bf16[256,1024]{1,0:T(8,128)(2,1)} %get-tuple-element.357.k_far.k_cross, ...), custom_call_target="tpu_custom_call" | custom-call | flops 4194304 | bytes 5242880 | tf_op jit(solution)/shard_map/cond/branch_1_fun/normalize/pallas_call | solution.py:48
  9.8 2.9 %collective-permute-start.13 = (bf16[256,2560]{1,0:T(8,128)(2,1)}, bf16[256,2560]{1,0:T(8,128)(2,1)}, u32[]{:S(2)}, u32[]{:S(2)}) collective-permute-start(bf16[256,2560]{1,0:T(8,128)(2,1)} %get-tuple-element.359), channel_id=1, source_target_pairs={{0,2},{1,3},{2,0},{3,1},{4,6},{5,7},{6,4},{7,5},{8,10},{9,11},{10,... | collective-permute-start | bytes 3932168 | tf_op jit(solution)/shard_map/cond/branch_1_fun/ppermute | solution.py:368
  12.8 21.0 %conditional.3 = ((bf16[256,8448]{1,0:T(8,128)(2,1)}, bf16[256,8448]{1,0:T(8,128)(2,1)}, bf16[256,512]{1,0:T(8,128)(2,1)S(1)})) conditional(s32[]{:T(128)} %convert_element_type.13, () %tuple.98, (s32[1]{0:T(128)}, bf16[256,2560]{1,0:T(8,128)(2,1)}, bf16[256,2048]{1,0:T(8,128)(2,1)}, bf16[256,4096]{1,0:T(8,128)(2,1)}, ...), branch_computations={%region_8.8_spmd, %region_9.9_spmd} | conditional | flops 1073741824 | bytes 49545316 | solution.py:352
  12.8 2.7 %pack.6.refs_0_ = bf16[256,8448]{1,0:T(8,128)(2,1)S(1)} custom-call(s32[1]{0:T(128)} %get-tuple-element.330.place, bf16[256,2560]{1,0:T(8,128)(2,1)} %get-tuple-element.331.refs_0_, bf16[256,2048]{1,0:T(8,128)(2,1)} %get-tuple-element.332.refs_1_, bf16[256,4096]{1,0:T(8,128)(2,1)} %get-tuple-element.333.refs_2_.refs_1_, ...), custom_call_target="tpu_custom_call" | custom-call | bytes 8650752 | tf_op jit(solution)/shard_map/cond/branch_1_fun/cond/branch_1_fun/pack/pallas_call | solution.py:93
  19.1 7.1 %collective-permute-done.9.refs_2_ = bf16[256,8448]{1,0:T(8,128)(2,1)} collective-permute-done((bf16[256,8448]{1,0:T(8,128)(2,1)S(1)}, bf16[256,8448]{1,0:T(8,128)(2,1)}, u32[]{:S(2)}, u32[]{:S(2)}) %collective-permute-start.9) | collective-permute-done | bytes 4325408 | tf_op jit(solution)/shard_map/cond/branch_1_fun/cond/branch_1_fun/ppermute | solution.py:368
  26.2 7.6 %project.12 = bf16[256,512]{1,0:T(8,128)(2,1)S(1)} custom-call(bf16[256,8448]{1,0:T(8,128)(2,1)} %copy-done.7, bf16[256,4096]{1,0:T(8,128)(2,1)} %get-tuple-element.333.refs_2_.refs_1_, bf16[256,8448]{1,0:T(8,128)(2,1)} %collective-permute-done.9.refs_2_), custom_call_target="tpu_custom_call" | custom-call | flops 1073741824 | bytes 6291456 | tf_op jit(solution)/shard_map/cond/branch_1_fun/cond/branch_1_fun/project/pallas_call | solution.py:216
  33.8 7.2 %collective-permute-done.13.refs_0_ = bf16[256,2560]{1,0:T(8,128)(2,1)} collective-permute-done((bf16[256,2560]{1,0:T(8,128)(2,1)}, bf16[256,2560]{1,0:T(8,128)(2,1)}, u32[]{:S(2)}, u32[]{:S(2)}) %collective-permute-start.13) | collective-permute-done | bytes 1310752 | tf_op jit(solution)/shard_map/cond/branch_1_fun/ppermute | solution.py:368
  41.0 12.6 %conditional.4 = ((f32[256,2048]{1,0:T(8,128)}, bf16[256,2048]{1,0:T(8,128)(2,1)}, bf16[256,2560]{1,0:T(8,128)(2,1)})) conditional(s32[]{:T(128)} %convert_element_type.13, () %tuple.97, (bf16[256,2560]{1,0:T(8,128)(2,1)}, s32[1]{0:T(128)}, bf16[256,1024]{1,0:T(8,128)(2,1)S(1)}, bf16[256,8448]{1,0:T(8,128)(2,1)}, bf16[256,8448]{1,0:T(8,128)(2,1)}, ...), branch_computations={%region_10.10_spmd, %region_11.11_spmd} | conditional | flops 1073741824 | bytes 13631560 | solution.py:352
  41.0 3.3 %collective-permute-start.10 = (bf16[256,2560]{1,0:T(8,128)(2,1)}, bf16[256,2560]{1,0:T(8,128)(2,1)}, u32[]{:S(2)}, u32[]{:S(2)}) collective-permute-start(bf16[256,2560]{1,0:T(8,128)(2,1)} %get-tuple-element.338.k_far.n_far), channel_id=1, source_target_pairs={{0,1},{1,0},{2,3},{3,2},{4,5},{5,4},{6,7},{7,6},{8,9},{9,8},{10,11... | collective-permute-start | bytes 3932168 | tf_op jit(solution)/shard_map/cond/branch_1_fun/cond/branch_1_fun/ppermute | solution.py:368
  44.3 3.0 %collective-permute-done.10.k_cross.n_cross = bf16[256,2560]{1,0:T(8,128)(2,1)} collective-permute-done((bf16[256,2560]{1,0:T(8,128)(2,1)}, bf16[256,2560]{1,0:T(8,128)(2,1)}, u32[]{:S(2)}, u32[]{:S(2)}) %collective-permute-start.10) | collective-permute-done | bytes 1310752 | tf_op jit(solution)/shard_map/cond/branch_1_fun/cond/branch_1_fun/ppermute | solution.py:368
  47.3 6.3 %moment_part.12 = (f32[256,2048]{1,0:T(8,128)}, bf16[256,2048]{1,0:T(8,128)(2,1)}) custom-call(s32[1]{0:T(128)} %get-tuple-element.335.place, bf16[256,1024]{1,0:T(8,128)(2,1)S(1)} %get-tuple-element.336.k_own, bf16[256,8448]{1,0:T(8,128)(2,1)} %get-tuple-element.337.k_sib.n_sib, bf16[256,2560]{1,0:T(8,128)(2,1)} %get-tuple-element.338.k_far.n_far, ...), custom_call_target="tpu_custom_call" | custom-call | flops 1073741824 | bytes 8388608 | tf_op jit(solution)/shard_map/cond/branch_1_fun/cond/branch_1_fun/moment_part/pallas_call | solution.py:144
  55.6 7.8 %collective-permute-done.12.refs_1_ = bf16[256,2048]{1,0:T(8,128)(2,1)} collective-permute-done((bf16[256,2048]{1,0:T(8,128)(2,1)}, bf16[256,2048]{1,0:T(8,128)(2,1)}, u32[]{:S(2)}, u32[]{:S(2)}) %collective-permute-start.12) | collective-permute-done | bytes 1048608 | tf_op jit(solution)/shard_map/cond/branch_1_fun/ppermute | solution.py:368
  63.4 10.8 %conditional.5 = ((f32[256,2048]{1,0:T(8,128)}, bf16[256,2048]{1,0:T(8,128)(2,1)})) conditional(s32[]{:T(128)} %convert_element_type.13, () %tuple.96, (bf16[256,2048]{1,0:T(8,128)(2,1)}, s32[1]{0:T(128)}, bf16[256,1024]{1,0:T(8,128)(2,1)S(1)}, bf16[256,8448]{1,0:T(8,128)(2,1)}, bf16[256,2560]{1,0:T(8,128)(2,1)}, ...), branch_computations={%region_12.12_spmd, %region_13.13_spmd} | conditional | flops 1073741824 | bytes 12582960 | solution.py:352
  65.3 2.6 %collective-permute-done.11.n_cross = bf16[256,2048]{1,0:T(8,128)(2,1)} collective-permute-done((bf16[256,2048]{1,0:T(8,128)(2,1)}, bf16[256,2048]{1,0:T(8,128)(2,1)}, u32[]{:S(2)}, u32[]{:S(2)}) %collective-permute-start.11) | collective-permute-done | bytes 1048608 | tf_op jit(solution)/shard_map/cond/branch_1_fun/cond/branch_1_fun/ppermute | solution.py:368
  67.9 6.3 %moment_part.13 = (f32[256,2048]{1,0:T(8,128)}, bf16[256,2048]{1,0:T(8,128)(2,1)}) custom-call(s32[1]{0:T(128)} %get-tuple-element.345.place, bf16[256,1024]{1,0:T(8,128)(2,1)S(1)} %get-tuple-element.346.k_own, bf16[256,8448]{1,0:T(8,128)(2,1)} %get-tuple-element.347.k_sib.n_sib, bf16[256,2560]{1,0:T(8,128)(2,1)} %get-tuple-element.348.k_far, ...), custom_call_target="tpu_custom_call" | custom-call | flops 1073741824 | bytes 8388608 | tf_op jit(solution)/shard_map/cond/branch_1_fun/cond/branch_1_fun/moment_part/pallas_call | solution.py:144
  74.4 8.4 %project.13 = bf16[256,512]{1,0:T(8,128)(2,1)} custom-call(bf16[256,2560]{1,0:T(8,128)(2,1)} %collective-permute-done.13.refs_0_, bf16[256,2048]{1,0:T(8,128)(2,1)} %collective-permute-done.12.refs_1_, bf16[256,4096]{1,0:T(8,128)(2,1)} %get-tuple-element.360.refs_2_.weights, bf16[256,8448]{1,0:T(8,128)(2,1)} %get-tuple-element.363.refs_3_), custom_call_target="tpu_custom_call" | custom-call | flops 1073741824 | bytes 6291456 | tf_op jit(solution)/shard_map/cond/branch_1_fun/project/pallas_call | solution.py:216
  82.8 3.0 %collective-permute-start.17 = (bf16[256,512]{1,0:T(8,128)(2,1)}, bf16[256,512]{1,0:T(8,128)(2,1)S(1)}, u32[]{:S(2)}, u32[]{:S(2)}) collective-permute-start(bf16[256,512]{1,0:T(8,128)(2,1)} %project.13), channel_id=1, source_target_pairs={{0,2},{1,3},{2,0},{3,1},{4,6},{5,7},{6,4},{7,5},{8,10},{9,11},{10,... | collective-permute-start | bytes 786440 | tf_op jit(solution)/shard_map/cond/branch_1_fun/ppermute | solution.py:368
  85.8 3.7 %average_part.12 = (bf16[256,4096]{1,0:T(8,128)(2,1)}, bf16[256,4096]{1,0:T(8,128)(2,1)}) custom-call(f32[1]{0:T(128)} %get-tuple-element.374.rate, f32[256,2048]{1,0:T(8,128)} %get-tuple-element.375.new, bf16[256,2048]{1,0:T(8,128)(2,1)} %collective-permute-done.16.peer, bf16[256,4096]{1,0:T(8,128)(2,1)} %get-tuple-element.360.refs_2_.weights, ...), custom_call_target="tpu_custom_call" | custom-call | flops 3145728 | bytes 7340032 | tf_op jit(solution)/shard_map/cond/branch_1_fun/average_part/pallas_call | solution.py:321
  89.5 2.2 %collective-permute-done.17.refs_2_.refs_3_ = bf16[256,512]{1,0:T(8,128)(2,1)S(1)} collective-permute-done((bf16[256,512]{1,0:T(8,128)(2,1)}, bf16[256,512]{1,0:T(8,128)(2,1)S(1)}, u32[]{:S(2)}, u32[]{:S(2)}) %collective-permute-start.17) | collective-permute-done | bytes 262176 | tf_op jit(solution)/shard_map/cond/branch_1_fun/ppermute | solution.py:368
  92.4 2.6 %place_blocks.6 = bf16[256,1024]{1,0:T(8,128)(2,1)} custom-call(s32[1]{0:T(128)} %get-tuple-element.354.place, bf16[256,512]{1,0:T(8,128)(2,1)} %copy-done.18, bf16[256,512]{1,0:T(8,128)(2,1)} %copy-done.18, bf16[256,512]{1,0:T(8,128)(2,1)} %copy-done.13, bf16[256,512]{1,0:T(8,128)(2,1)} %copy-done.13), custom_call_target="tpu_custom_call" | custom-call | bytes 1048576 | tf_op jit(solution)/shard_map/cond/branch_1_fun/place_blocks/pallas_call | solution.py:249
  95.0 7.2 %collective-permute-done.15.peer = bf16[256,2048]{1,0:T(8,128)(2,1)S(1)} collective-permute-done((bf16[256,2048]{1,0:T(8,128)(2,1)}, bf16[256,2048]{1,0:T(8,128)(2,1)S(1)}, u32[]{:S(2)}, u32[]{:S(2)}) %collective-permute-start.15) | collective-permute-done | bytes 1048608 | tf_op jit(solution)/shard_map/cond/branch_1_fun/ppermute | solution.py:368
  102.2 3.3 %average_part.13 = (bf16[256,4096]{1,0:T(8,128)(2,1)}, bf16[256,4096]{1,0:T(8,128)(2,1)}) custom-call(f32[1]{0:T(128)} %get-tuple-element.374.rate, f32[256,2048]{1,0:T(8,128)} %get-tuple-element.382.new, bf16[256,2048]{1,0:T(8,128)(2,1)S(1)} %collective-permute-done.15.peer, ...), custom_call_target="tpu_custom_call", output_to_operand_aliasing={{0}: (5, {}), {1}: (6, {})} | custom-call | flops 3145728 | bytes 7340032 | tf_op jit(solution)/shard_map/cond/branch_1_fun/average_part/pallas_call | solution.py:321
  (15 shorter events, 8.5 us)
Async XLA Ops:
  1.3 11.5 %copy-start.2 = (bf16[256,1024]{1,0:T(8,128)(2,1)S(1)}, bf16[256,1024]{1,0:T(8,128)(2,1)}, u32[]{:S(2)}) copy-start(bf16[256,1024]{1,0:T(8,128)(2,1)} %get-tuple-element.357.k_far.k_cross) | copy-start | bytes 1572868 | tf_op jit(solution)/shard_map/cond
  1.3 52.2 %collective-permute-start.14 = (bf16[256,4096]{1,0:T(8,128)(2,1)}, bf16[256,4096]{1,0:T(8,128)(2,1)S(1)}, u32[]{:S(2)}, u32[]{:S(2)}) collective-permute-start(bf16[256,4096]{1,0:T(8,128)(2,1)} %get-tuple-element.360.refs_2_.weights), channel_id=1, source_target_pairs={{0,8},{1,9},{2,10},{3,11},{4,12},{5,13},{6,14},{7,15},{8,0},{9,1},... | collective-permute-start | bytes 6291464 | tf_op jit(solution)/shard_map/cond/branch_1_fun/ppermute | solution.py:368
  9.8 31.1 %collective-permute-start.13 = (bf16[256,2560]{1,0:T(8,128)(2,1)}, bf16[256,2560]{1,0:T(8,128)(2,1)}, u32[]{:S(2)}, u32[]{:S(2)}) collective-permute-start(bf16[256,2560]{1,0:T(8,128)(2,1)} %get-tuple-element.359), channel_id=1, source_target_pairs={{0,2},{1,3},{2,0},{3,1},{4,6},{5,7},{6,4},{7,5},{8,10},{9,11},{10,... | collective-permute-start | bytes 3932168 | tf_op jit(solution)/shard_map/cond/branch_1_fun/ppermute | solution.py:368
  12.7 50.7 %collective-permute-start.12 = (bf16[256,2048]{1,0:T(8,128)(2,1)}, bf16[256,2048]{1,0:T(8,128)(2,1)}, u32[]{:S(2)}, u32[]{:S(2)}) collective-permute-start(bf16[256,2048]{1,0:T(8,128)(2,1)} %get-tuple-element.358), channel_id=1, source_target_pairs={{0,2},{1,3},{2,0},{3,1},{4,6},{5,7},{6,4},{7,5},{8,10},{9,11},{10,... | collective-permute-start | bytes 3145736 | tf_op jit(solution)/shard_map/cond/branch_1_fun/ppermute | solution.py:368
  15.5 2.1 %copy-start.7 = (bf16[256,8448]{1,0:T(8,128)(2,1)}, bf16[256,8448]{1,0:T(8,128)(2,1)S(1)}, u32[]{:S(2)}) copy-start(bf16[256,8448]{1,0:T(8,128)(2,1)S(1)} %pack.6.refs_0_) | copy-start | bytes 12976132 | tf_op jit(solution)/shard_map/cond/branch_1_fun/cond
  17.6 8.6 %collective-permute-start.9 = (bf16[256,8448]{1,0:T(8,128)(2,1)S(1)}, bf16[256,8448]{1,0:T(8,128)(2,1)}, u32[]{:S(2)}, u32[]{:S(2)}) collective-permute-start(bf16[256,8448]{1,0:T(8,128)(2,1)S(1)} %pack.6.refs_0_), channel_id=1, source_target_pairs={{0,1},{1,0},{2,3},{3,2},{4,5},{5,4},{6,7},{7,6},{8,9},{9,8},{10,11... | collective-permute-start | bytes 12976136 | tf_op jit(solution)/shard_map/cond/branch_1_fun/cond/branch_1_fun/ppermute | solution.py:368
  33.8 7.2 %copy-start.18 = (bf16[256,512]{1,0:T(8,128)(2,1)}, bf16[256,512]{1,0:T(8,128)(2,1)S(1)}, u32[]{:S(2)}) copy-start(bf16[256,512]{1,0:T(8,128)(2,1)S(1)} %get-tuple-element.371.refs_0_.refs_1_) | copy-start | bytes 786436 | tf_op jit(solution)/shard_map/cond
  41.0 6.3 %collective-permute-start.10 = (bf16[256,2560]{1,0:T(8,128)(2,1)}, bf16[256,2560]{1,0:T(8,128)(2,1)}, u32[]{:S(2)}, u32[]{:S(2)}) collective-permute-start(bf16[256,2560]{1,0:T(8,128)(2,1)} %get-tuple-element.338.k_far.n_far), channel_id=1, source_target_pairs={{0,1},{1,0},{2,3},{3,2},{4,5},{5,4},{6,7},{7,6},{8,9},{9,8},{10,11... | collective-permute-start | bytes 3932168 | tf_op jit(solution)/shard_map/cond/branch_1_fun/cond/branch_1_fun/ppermute | solution.py:368
  53.6 29.2 %collective-permute-start.16 = (bf16[256,2048]{1,0:T(8,128)(2,1)}, bf16[256,2048]{1,0:T(8,128)(2,1)}, u32[]{:S(2)}, u32[]{:S(2)}) collective-permute-start(bf16[256,2048]{1,0:T(8,128)(2,1)} %get-tuple-element.367), channel_id=1, source_target_pairs={{0,8},{1,9},{2,10},{3,11},{4,12},{5,13},{6,14},{7,15},{8,0},{9,1},... | collective-permute-start | bytes 3145736 | tf_op jit(solution)/shard_map/cond/branch_1_fun/ppermute | solution.py:368
  63.4 4.5 %collective-permute-start.11 = (bf16[256,2048]{1,0:T(8,128)(2,1)}, bf16[256,2048]{1,0:T(8,128)(2,1)}, u32[]{:S(2)}, u32[]{:S(2)}) collective-permute-start(bf16[256,2048]{1,0:T(8,128)(2,1)} %get-tuple-element.351.n_far), channel_id=1, source_target_pairs={{0,1},{1,0},{2,3},{3,2},{4,5},{5,4},{6,7},{7,6},{8,9},{9,8},{10,11... | collective-permute-start | bytes 3145736 | tf_op jit(solution)/shard_map/cond/branch_1_fun/cond/branch_1_fun/ppermute | solution.py:368
  74.3 27.9 %collective-permute-start.15 = (bf16[256,2048]{1,0:T(8,128)(2,1)}, bf16[256,2048]{1,0:T(8,128)(2,1)S(1)}, u32[]{:S(2)}, u32[]{:S(2)}) collective-permute-start(bf16[256,2048]{1,0:T(8,128)(2,1)} %get-tuple-element.370), channel_id=1, source_target_pairs={{0,8},{1,9},{2,10},{3,11},{4,12},{5,13},{6,14},{7,15},{8,0},{9,1},... | collective-permute-start | bytes 3145736 | tf_op jit(solution)/shard_map/cond/branch_1_fun/ppermute | solution.py:368
  82.8 8.9 %collective-permute-start.17 = (bf16[256,512]{1,0:T(8,128)(2,1)}, bf16[256,512]{1,0:T(8,128)(2,1)S(1)}, u32[]{:S(2)}, u32[]{:S(2)}) collective-permute-start(bf16[256,512]{1,0:T(8,128)(2,1)} %project.13), channel_id=1, source_target_pairs={{0,2},{1,3},{2,0},{3,1},{4,6},{5,7},{6,4},{7,5},{8,10},{9,11},{10,... | collective-permute-start | bytes 786440 | tf_op jit(solution)/shard_map/cond/branch_1_fun/ppermute | solution.py:368
  91.7 0.7 copy-start.13
where the time goes:
time: 107 us; the launch traced here: 106 us
  Pallas kernels  45.7 us (43%)
  waiting for transfers between devices  37.2 us (35%)
  starting transfers between devices  18.5 us (17%)
  local copies, waits for them, and re-layouts  2.79 us (3%)
  between operations  1.46 us (1%)
    ppermute x9, waiting for transfers between devices, move(): return lax.ppermute(value, AXES, pairs)  37.2 us
    ppermute x9, starting transfers between devices, move(): return lax.ppermute(value, AXES, pairs)  18.5 us
    pallas_call x2, Pallas kernels, project(): pl.pallas_call(partial(project_kernel, scale, per), grid=(tiles,), in_spe...  15.9 us
    pallas_call x2, Pallas kernels, moment_part(): pl.pallas_call(partial(moment_kernel, scale, 256), grid_spec=pltpu.Prefet...  12.6 us
    pallas_call x2, Pallas kernels, average_part(): pl.pallas_call(partial(average_kernel, start), in_specs=[pl.BlockSpec(mem...  7.04 us
    pallas_call x1, Pallas kernels, normalize(): pl.pallas_call(norm_kernel, grid_spec=pltpu.PrefetchScalarGridSpec(num_sc...  4.82 us
    cond x8, local copies, waits for them, and re-layouts  2.79 us
    pallas_call x1, Pallas kernels, pack(): pl.pallas_call(pack_kernel, in_specs=[pl.BlockSpec(memory_space=pltpu.SME...  2.73 us
  transfers between devices with their start and end apart: 9, of which 7 were waited for; matrix products, arithmetic and copies ran while one was open for 0% of the time, Pallas kernels for 40%

commit v1 on v0

--- a/solution.py
+++ b/solution.py
@@ -130,7 +130,7 @@
 def moment_part(scale, place, grads, own, sib, far, cross, first, moments, start, columns):
     rows, model = moments.shape
     tokens = own.shape[0]
-    tile = 512
+    tile = 1024
     k_specs = [
         pl.BlockSpec((tokens, rows), lambda i, p: (0, p[0])),
         pl.BlockSpec((tokens, rows), lambda i, p: (0, 2 * model // rows)),
@@ -265,7 +265,7 @@
 def average_kernel(start, rate, new, peer, weights, peer_weights, *refs):
     weight_out, moment_out, n_buf, p_buf, w_buf, q_buf, wo_buf, mo_buf, in_sems, out_sems = refs[-10:]
     tiles, rows, tile = n_buf.shape
-    step = 32
+    step = 64
 
     def columns(t, start):
         return pl.ds(pl.multiple_of(start + t * tile, tile), tile)
@@ -429,7 +429,7 @@
     place = lax.axis_index("fsdp").reshape(1)
     branches = [partial(branch, bit, reps, shards) for bit in range(levels)]
     outs = lax.switch(
-        step[0] % levels,
+        lax.rem(step[0], levels),
         branches,
         tokens[0],
         gain,

time: 107 us -> 106 us (level)
  no operation moved by 1% of the time
where the time goes in v1:
time: 106 us; the launch traced here: 105 us
  Pallas kernels  44.8 us (42%)
  waiting for transfers between devices  37.5 us (35%)
  starting transfers between devices  18.6 us (18%)
  local copies, waits for them, and re-layouts  2.79 us (3%)
  between operations  1.45 us (1%)
    ppermute x9, waiting for transfers between devices, move(): return lax.ppermute(value, AXES, pairs)  37.5 us
    ppermute x9, starting transfers between devices, move(): return lax.ppermute(value, AXES, pairs)  18.6 us
    pallas_call x2, Pallas kernels, project(): pl.pallas_call(partial(project_kernel, scale, per), grid=(tiles,), in_spe...  15.9 us
    pallas_call x2, Pallas kernels, moment_part(): pl.pallas_call(partial(moment_kernel, scale, 256), grid_spec=pltpu.Prefet...  12 us
    pallas_call x2, Pallas kernels, average_part(): pl.pallas_call(partial(average_kernel, start), in_specs=[pl.BlockSpec(mem...  6.85 us
    pallas_call x1, Pallas kernels, normalize(): pl.pallas_call(norm_kernel, grid_spec=pltpu.PrefetchScalarGridSpec(num_sc...  4.82 us
    cond x8, local copies, waits for them, and re-layouts  2.79 us
    pallas_call x1, Pallas kernels, pack(): pl.pallas_call(pack_kernel, in_specs=[pl.BlockSpec(memory_space=pltpu.SME...  2.73 us
  transfers between devices with their start and end apart: 9, of which 7 were waited for; matrix products, arithmetic and copies ran while one was open for 0% of the time, Pallas kernels for 40%

profile of v1, /device:TPU:1, one launch (start us, length us, event | category | flops | bytes accessed | tf_op | source)
XLA Modules:
  0.0 105.4 jit_solution(9251175447152003123)
XLA Ops:
  1.3 104.0 %conditional.16 = (bf16[256,1024]{1,0:T(8,128)(2,1)}, bf16[256,4096]{1,0:T(8,128)(2,1)}, bf16[256,4096]{1,0:T(8,128)(2,1)}) conditional(s32[]{:T(128)} %bitcast, (pred[]{:T(512)}, s32[1]{0:T(128)}, bf16[256,4096]{1,0:T(8,128)(2,1)}, f32[1,4096]{1,0:T(1,128)}, bf16[256,1024]{1,0:T(8,128)(2,1)}, ...), branch_computations={%region_0.0_spmd, %region_7.0_spmd, %region_14.0_spmd, %region_21.... | conditional | flops 4305453056 | bytes 154403648 | solution.py:431
  1.3 3.7 %collective-permute-start.14 = (bf16[256,4096]{1,0:T(8,128)(2,1)}, bf16[256,4096]{1,0:T(8,128)(2,1)S(1)}, u32[]{:S(2)}, u32[]{:S(2)}) collective-permute-start(bf16[256,4096]{1,0:T(8,128)(2,1)} %get-tuple-element.360.refs_2_.weights), channel_id=1, source_target_pairs={{0,8},{1,9},{2,10},{3,11},{4,12},{5,13},{6,14},{7,15},{8,0},{9,1},... | collective-permute-start | bytes 6291464 | tf_op jit(solution)/shard_map/cond/branch_1_fun/ppermute | solution.py:368
  5.0 4.8 %normalize.6 = (bf16[256,2560]{1,0:T(8,128)(2,1)}, bf16[256,2048]{1,0:T(8,128)(2,1)}) custom-call(s32[1]{0:T(128)} %get-tuple-element.354.place, bf16[256,4096]{1,0:T(8,128)(2,1)} %get-tuple-element.355.tok, f32[1,4096]{1,0:T(1,128)} %get-tuple-element.356.gains, bf16[256,1024]{1,0:T(8,128)(2,1)} %get-tuple-element.357.k_far.k_cross, ...), custom_call_target="tpu_custom_call" | custom-call | flops 4194304 | bytes 5242880 | tf_op jit(solution)/shard_map/cond/branch_1_fun/normalize/pallas_call | solution.py:48
  9.8 2.9 %collective-permute-start.13 = (bf16[256,2560]{1,0:T(8,128)(2,1)}, bf16[256,2560]{1,0:T(8,128)(2,1)}, u32[]{:S(2)}, u32[]{:S(2)}) collective-permute-start(bf16[256,2560]{1,0:T(8,128)(2,1)} %get-tuple-element.359), channel_id=1, source_target_pairs={{0,2},{1,3},{2,0},{3,1},{4,6},{5,7},{6,4},{7,5},{8,10},{9,11},{10,... | collective-permute-start | bytes 3932168 | tf_op jit(solution)/shard_map/cond/branch_1_fun/ppermute | solution.py:368
  12.8 21.0 %conditional.3 = ((bf16[256,8448]{1,0:T(8,128)(2,1)}, bf16[256,8448]{1,0:T(8,128)(2,1)}, bf16[256,512]{1,0:T(8,128)(2,1)S(1)})) conditional(s32[]{:T(128)} %convert_element_type.13, () %tuple.98, (s32[1]{0:T(128)}, bf16[256,2560]{1,0:T(8,128)(2,1)}, bf16[256,2048]{1,0:T(8,128)(2,1)}, bf16[256,4096]{1,0:T(8,128)(2,1)}, ...), branch_computations={%region_8.0_spmd, %region_9.0_spmd} | conditional | flops 1073741824 | bytes 49545316 | solution.py:352
  12.8 2.7 %pack.6.refs_0_ = bf16[256,8448]{1,0:T(8,128)(2,1)S(1)} custom-call(s32[1]{0:T(128)} %get-tuple-element.330.place, bf16[256,2560]{1,0:T(8,128)(2,1)} %get-tuple-element.331.refs_0_, bf16[256,2048]{1,0:T(8,128)(2,1)} %get-tuple-element.332.refs_1_, bf16[256,4096]{1,0:T(8,128)(2,1)} %get-tuple-element.333.refs_2_.refs_1_, ...), custom_call_target="tpu_custom_call" | custom-call | bytes 8650752 | tf_op jit(solution)/shard_map/cond/branch_1_fun/cond/branch_1_fun/pack/pallas_call | solution.py:93
  19.1 7.1 %collective-permute-done.9.refs_2_ = bf16[256,8448]{1,0:T(8,128)(2,1)} collective-permute-done((bf16[256,8448]{1,0:T(8,128)(2,1)S(1)}, bf16[256,8448]{1,0:T(8,128)(2,1)}, u32[]{:S(2)}, u32[]{:S(2)}) %collective-permute-start.9) | collective-permute-done | bytes 4325408 | tf_op jit(solution)/shard_map/cond/branch_1_fun/cond/branch_1_fun/ppermute | solution.py:368
  26.2 7.5 %project.12 = bf16[256,512]{1,0:T(8,128)(2,1)S(1)} custom-call(bf16[256,8448]{1,0:T(8,128)(2,1)} %copy-done.7, bf16[256,4096]{1,0:T(8,128)(2,1)} %get-tuple-element.333.refs_2_.refs_1_, bf16[256,8448]{1,0:T(8,128)(2,1)} %collective-permute-done.9.refs_2_), custom_call_target="tpu_custom_call" | custom-call | flops 1073741824 | bytes 6291456 | tf_op jit(solution)/shard_map/cond/branch_1_fun/cond/branch_1_fun/project/pallas_call | solution.py:216
  33.8 7.2 %collective-permute-done.13.refs_0_ = bf16[256,2560]{1,0:T(8,128)(2,1)} collective-permute-done((bf16[256,2560]{1,0:T(8,128)(2,1)}, bf16[256,2560]{1,0:T(8,128)(2,1)}, u32[]{:S(2)}, u32[]{:S(2)}) %collective-permute-start.13) | collective-permute-done | bytes 1310752 | tf_op jit(solution)/shard_map/cond/branch_1_fun/ppermute | solution.py:368
  41.0 12.3 %conditional.4 = ((f32[256,2048]{1,0:T(8,128)}, bf16[256,2048]{1,0:T(8,128)(2,1)}, bf16[256,2560]{1,0:T(8,128)(2,1)})) conditional(s32[]{:T(128)} %convert_element_type.13, () %tuple.97, (bf16[256,2560]{1,0:T(8,128)(2,1)}, s32[1]{0:T(128)}, bf16[256,1024]{1,0:T(8,128)(2,1)S(1)}, bf16[256,8448]{1,0:T(8,128)(2,1)}, bf16[256,8448]{1,0:T(8,128)(2,1)}, ...), branch_computations={%region_10.0_spmd, %region_11.0_spmd} | conditional | flops 1073741824 | bytes 13631560 | solution.py:352
  41.0 3.3 %collective-permute-start.10 = (bf16[256,2560]{1,0:T(8,128)(2,1)}, bf16[256,2560]{1,0:T(8,128)(2,1)}, u32[]{:S(2)}, u32[]{:S(2)}) collective-permute-start(bf16[256,2560]{1,0:T(8,128)(2,1)} %get-tuple-element.338.k_far.n_far), channel_id=1, source_target_pairs={{0,1},{1,0},{2,3},{3,2},{4,5},{5,4},{6,7},{7,6},{8,9},{9,8},{10,11... | collective-permute-start | bytes 3932168 | tf_op jit(solution)/shard_map/cond/branch_1_fun/cond/branch_1_fun/ppermute | solution.py:368
  44.3 3.0 %collective-permute-done.10.k_cross.n_cross = bf16[256,2560]{1,0:T(8,128)(2,1)} collective-permute-done((bf16[256,2560]{1,0:T(8,128)(2,1)}, bf16[256,2560]{1,0:T(8,128)(2,1)}, u32[]{:S(2)}, u32[]{:S(2)}) %collective-permute-start.10) | collective-permute-done | bytes 1310752 | tf_op jit(solution)/shard_map/cond/branch_1_fun/cond/branch_1_fun/ppermute | solution.py:368
  47.3 6.0 %moment_part.12 = (f32[256,2048]{1,0:T(8,128)}, bf16[256,2048]{1,0:T(8,128)(2,1)}) custom-call(s32[1]{0:T(128)} %get-tuple-element.335.place, bf16[256,1024]{1,0:T(8,128)(2,1)S(1)} %get-tuple-element.336.k_own, bf16[256,8448]{1,0:T(8,128)(2,1)} %get-tuple-element.337.k_sib.n_sib, bf16[256,2560]{1,0:T(8,128)(2,1)} %get-tuple-element.338.k_far.n_far, ...), custom_call_target="tpu_custom_call" | custom-call | flops 1073741824 | bytes 8388608 | tf_op jit(solution)/shard_map/cond/branch_1_fun/cond/branch_1_fun/moment_part/pallas_call | solution.py:144
  55.3 8.1 %collective-permute-done.12.refs_1_ = bf16[256,2048]{1,0:T(8,128)(2,1)} collective-permute-done((bf16[256,2048]{1,0:T(8,128)(2,1)}, bf16[256,2048]{1,0:T(8,128)(2,1)}, u32[]{:S(2)}, u32[]{:S(2)}) %collective-permute-start.12) | collective-permute-done | bytes 1048608 | tf_op jit(solution)/shard_map/cond/branch_1_fun/ppermute | solution.py:368
  63.4 10.5 %conditional.5 = ((f32[256,2048]{1,0:T(8,128)}, bf16[256,2048]{1,0:T(8,128)(2,1)})) conditional(s32[]{:T(128)} %convert_element_type.13, () %tuple.96, (bf16[256,2048]{1,0:T(8,128)(2,1)}, s32[1]{0:T(128)}, bf16[256,1024]{1,0:T(8,128)(2,1)S(1)}, bf16[256,8448]{1,0:T(8,128)(2,1)}, bf16[256,2560]{1,0:T(8,128)(2,1)}, ...), branch_computations={%region_12.0_spmd, %region_13.0_spmd} | conditional | flops 1073741824 | bytes 12582960 | solution.py:352
  65.3 2.6 %collective-permute-done.11.n_cross = bf16[256,2048]{1,0:T(8,128)(2,1)} collective-permute-done((bf16[256,2048]{1,0:T(8,128)(2,1)}, bf16[256,2048]{1,0:T(8,128)(2,1)}, u32[]{:S(2)}, u32[]{:S(2)}) %collective-permute-start.11) | collective-permute-done | bytes 1048608 | tf_op jit(solution)/shard_map/cond/branch_1_fun/cond/branch_1_fun/ppermute | solution.py:368
  67.9 6.0 %moment_part.13 = (f32[256,2048]{1,0:T(8,128)}, bf16[256,2048]{1,0:T(8,128)(2,1)}) custom-call(s32[1]{0:T(128)} %get-tuple-element.345.place, bf16[256,1024]{1,0:T(8,128)(2,1)S(1)} %get-tuple-element.346.k_own, bf16[256,8448]{1,0:T(8,128)(2,1)} %get-tuple-element.347.k_sib.n_sib, bf16[256,2560]{1,0:T(8,128)(2,1)} %get-tuple-element.348.k_far, ...), custom_call_target="tpu_custom_call" | custom-call | flops 1073741824 | bytes 8388608 | tf_op jit(solution)/shard_map/cond/branch_1_fun/cond/branch_1_fun/moment_part/pallas_call | solution.py:144
  74.1 8.4 %project.13 = bf16[256,512]{1,0:T(8,128)(2,1)} custom-call(bf16[256,2560]{1,0:T(8,128)(2,1)} %collective-permute-done.13.refs_0_, bf16[256,2048]{1,0:T(8,128)(2,1)} %collective-permute-done.12.refs_1_, bf16[256,4096]{1,0:T(8,128)(2,1)} %get-tuple-element.360.refs_2_.weights, bf16[256,8448]{1,0:T(8,128)(2,1)} %get-tuple-element.363.refs_3_), custom_call_target="tpu_custom_call" | custom-call | flops 1073741824 | bytes 6291456 | tf_op jit(solution)/shard_map/cond/branch_1_fun/project/pallas_call | solution.py:216
  82.5 3.0 %collective-permute-start.17 = (bf16[256,512]{1,0:T(8,128)(2,1)}, bf16[256,512]{1,0:T(8,128)(2,1)S(1)}, u32[]{:S(2)}, u32[]{:S(2)}) collective-permute-start(bf16[256,512]{1,0:T(8,128)(2,1)} %project.13), channel_id=1, source_target_pairs={{0,2},{1,3},{2,0},{3,1},{4,6},{5,7},{6,4},{7,5},{8,10},{9,11},{10,... | collective-permute-start | bytes 786440 | tf_op jit(solution)/shard_map/cond/branch_1_fun/ppermute | solution.py:368
  85.5 3.7 %average_part.12 = (bf16[256,4096]{1,0:T(8,128)(2,1)}, bf16[256,4096]{1,0:T(8,128)(2,1)}) custom-call(f32[1]{0:T(128)} %get-tuple-element.374.rate, f32[256,2048]{1,0:T(8,128)} %get-tuple-element.375.new, bf16[256,2048]{1,0:T(8,128)(2,1)} %collective-permute-done.16.peer, bf16[256,4096]{1,0:T(8,128)(2,1)} %get-tuple-element.360.refs_2_.weights, ...), custom_call_target="tpu_custom_call" | custom-call | flops 3145728 | bytes 7340032 | tf_op jit(solution)/shard_map/cond/branch_1_fun/average_part/pallas_call | solution.py:321
  89.1 2.3 %collective-permute-done.17.refs_2_.refs_3_ = bf16[256,512]{1,0:T(8,128)(2,1)S(1)} collective-permute-done((bf16[256,512]{1,0:T(8,128)(2,1)}, bf16[256,512]{1,0:T(8,128)(2,1)S(1)}, u32[]{:S(2)}, u32[]{:S(2)}) %collective-permute-start.17) | collective-permute-done | bytes 262176 | tf_op jit(solution)/shard_map/cond/branch_1_fun/ppermute | solution.py:368
  92.1 2.6 %place_blocks.6 = bf16[256,1024]{1,0:T(8,128)(2,1)} custom-call(s32[1]{0:T(128)} %get-tuple-element.354.place, bf16[256,512]{1,0:T(8,128)(2,1)} %copy-done.18, bf16[256,512]{1,0:T(8,128)(2,1)} %copy-done.18, bf16[256,512]{1,0:T(8,128)(2,1)} %copy-done.13, bf16[256,512]{1,0:T(8,128)(2,1)} %copy-done.13), custom_call_target="tpu_custom_call" | custom-call | bytes 1048576 | tf_op jit(solution)/shard_map/cond/branch_1_fun/place_blocks/pallas_call | solution.py:249
  94.7 7.2 %collective-permute-done.15.peer = bf16[256,2048]{1,0:T(8,128)(2,1)S(1)} collective-permute-done((bf16[256,2048]{1,0:T(8,128)(2,1)}, bf16[256,2048]{1,0:T(8,128)(2,1)S(1)}, u32[]{:S(2)}, u32[]{:S(2)}) %collective-permute-start.15) | collective-permute-done | bytes 1048608 | tf_op jit(solution)/shard_map/cond/branch_1_fun/ppermute | solution.py:368
  101.9 3.2 %average_part.13 = (bf16[256,4096]{1,0:T(8,128)(2,1)}, bf16[256,4096]{1,0:T(8,128)(2,1)}) custom-call(f32[1]{0:T(128)} %get-tuple-element.374.rate, f32[256,2048]{1,0:T(8,128)} %get-tuple-element.382.new, bf16[256,2048]{1,0:T(8,128)(2,1)S(1)} %collective-permute-done.15.peer, ...), custom_call_target="tpu_custom_call", output_to_operand_aliasing={{0}: (5, {}), {1}: (6, {})} | custom-call | flops 3145728 | bytes 7340032 | tf_op jit(solution)/shard_map/cond/branch_1_fun/average_part/pallas_call | solution.py:321
  (15 shorter events, 8.5 us)
Async XLA Ops:
  1.3 11.5 %copy-start.2 = (bf16[256,1024]{1,0:T(8,128)(2,1)S(1)}, bf16[256,1024]{1,0:T(8,128)(2,1)}, u32[]{:S(2)}) copy-start(bf16[256,1024]{1,0:T(8,128)(2,1)} %get-tuple-element.357.k_far.k_cross) | copy-start | bytes 1572868 | tf_op jit(solution)/shard_map/cond
  1.3 51.9 %collective-permute-start.14 = (bf16[256,4096]{1,0:T(8,128)(2,1)}, bf16[256,4096]{1,0:T(8,128)(2,1)S(1)}, u32[]{:S(2)}, u32[]{:S(2)}) collective-permute-start(bf16[256,4096]{1,0:T(8,128)(2,1)} %get-tuple-element.360.refs_2_.weights), channel_id=1, source_target_pairs={{0,8},{1,9},{2,10},{3,11},{4,12},{5,13},{6,14},{7,15},{8,0},{9,1},... | collective-permute-start | bytes 6291464 | tf_op jit(solution)/shard_map/cond/branch_1_fun/ppermute | solution.py:368
  9.8 31.1 %collective-permute-start.13 = (bf16[256,2560]{1,0:T(8,128)(2,1)}, bf16[256,2560]{1,0:T(8,128)(2,1)}, u32[]{:S(2)}, u32[]{:S(2)}) collective-permute-start(bf16[256,2560]{1,0:T(8,128)(2,1)} %get-tuple-element.359), channel_id=1, source_target_pairs={{0,2},{1,3},{2,0},{3,1},{4,6},{5,7},{6,4},{7,5},{8,10},{9,11},{10,... | collective-permute-start | bytes 3932168 | tf_op jit(solution)/shard_map/cond/branch_1_fun/ppermute | solution.py:368
  12.7 50.7 %collective-permute-start.12 = (bf16[256,2048]{1,0:T(8,128)(2,1)}, bf16[256,2048]{1,0:T(8,128)(2,1)}, u32[]{:S(2)}, u32[]{:S(2)}) collective-permute-start(bf16[256,2048]{1,0:T(8,128)(2,1)} %get-tuple-element.358), channel_id=1, source_target_pairs={{0,2},{1,3},{2,0},{3,1},{4,6},{5,7},{6,4},{7,5},{8,10},{9,11},{10,... | collective-permute-start | bytes 3145736 | tf_op jit(solution)/shard_map/cond/branch_1_fun/ppermute | solution.py:368
  15.5 2.1 %copy-start.7 = (bf16[256,8448]{1,0:T(8,128)(2,1)}, bf16[256,8448]{1,0:T(8,128)(2,1)S(1)}, u32[]{:S(2)}) copy-start(bf16[256,8448]{1,0:T(8,128)(2,1)S(1)} %pack.6.refs_0_) | copy-start | bytes 12976132 | tf_op jit(solution)/shard_map/cond/branch_1_fun/cond
  17.6 8.6 %collective-permute-start.9 = (bf16[256,8448]{1,0:T(8,128)(2,1)S(1)}, bf16[256,8448]{1,0:T(8,128)(2,1)}, u32[]{:S(2)}, u32[]{:S(2)}) collective-permute-start(bf16[256,8448]{1,0:T(8,128)(2,1)S(1)} %pack.6.refs_0_), channel_id=1, source_target_pairs={{0,1},{1,0},{2,3},{3,2},{4,5},{5,4},{6,7},{7,6},{8,9},{9,8},{10,11... | collective-permute-start | bytes 12976136 | tf_op jit(solution)/shard_map/cond/branch_1_fun/cond/branch_1_fun/ppermute | solution.py:368
  33.8 7.2 %copy-start.18 = (bf16[256,512]{1,0:T(8,128)(2,1)}, bf16[256,512]{1,0:T(8,128)(2,1)S(1)}, u32[]{:S(2)}) copy-start(bf16[256,512]{1,0:T(8,128)(2,1)S(1)} %get-tuple-element.371.refs_0_.refs_1_) | copy-start | bytes 786436 | tf_op jit(solution)/shard_map/cond
  41.0 6.3 %collective-permute-start.10 = (bf16[256,2560]{1,0:T(8,128)(2,1)}, bf16[256,2560]{1,0:T(8,128)(2,1)}, u32[]{:S(2)}, u32[]{:S(2)}) collective-permute-start(bf16[256,2560]{1,0:T(8,128)(2,1)} %get-tuple-element.338.k_far.n_far), channel_id=1, source_target_pairs={{0,1},{1,0},{2,3},{3,2},{4,5},{5,4},{6,7},{7,6},{8,9},{9,8},{10,11... | collective-permute-start | bytes 3932168 | tf_op jit(solution)/shard_map/cond/branch_1_fun/cond/branch_1_fun/ppermute | solution.py:368
  53.3 29.2 %collective-permute-start.16 = (bf16[256,2048]{1,0:T(8,128)(2,1)}, bf16[256,2048]{1,0:T(8,128)(2,1)}, u32[]{:S(2)}, u32[]{:S(2)}) collective-permute-start(bf16[256,2048]{1,0:T(8,128)(2,1)} %get-tuple-element.367), channel_id=1, source_target_pairs={{0,8},{1,9},{2,10},{3,11},{4,12},{5,13},{6,14},{7,15},{8,0},{9,1},... | collective-permute-start | bytes 3145736 | tf_op jit(solution)/shard_map/cond/branch_1_fun/ppermute | solution.py:368
  63.4 4.5 %collective-permute-start.11 = (bf16[256,2048]{1,0:T(8,128)(2,1)}, bf16[256,2048]{1,0:T(8,128)(2,1)}, u32[]{:S(2)}, u32[]{:S(2)}) collective-permute-start(bf16[256,2048]{1,0:T(8,128)(2,1)} %get-tuple-element.351.n_far), channel_id=1, source_target_pairs={{0,1},{1,0},{2,3},{3,2},{4,5},{5,4},{6,7},{7,6},{8,9},{9,8},{10,11... | collective-permute-start | bytes 3145736 | tf_op jit(solution)/shard_map/cond/branch_1_fun/cond/branch_1_fun/ppermute | solution.py:368
  73.9 28.0 %collective-permute-start.15 = (bf16[256,2048]{1,0:T(8,128)(2,1)}, bf16[256,2048]{1,0:T(8,128)(2,1)S(1)}, u32[]{:S(2)}, u32[]{:S(2)}) collective-permute-start(bf16[256,2048]{1,0:T(8,128)(2,1)} %get-tuple-element.370), channel_id=1, source_target_pairs={{0,8},{1,9},{2,10},{3,11},{4,12},{5,13},{6,14},{7,15},{8,0},{9,1},... | collective-permute-start | bytes 3145736 | tf_op jit(solution)/shard_map/cond/branch_1_fun/ppermute | solution.py:368
  82.5 8.9 %collective-permute-start.17 = (bf16[256,512]{1,0:T(8,128)(2,1)}, bf16[256,512]{1,0:T(8,128)(2,1)S(1)}, u32[]{:S(2)}, u32[]{:S(2)}) collective-permute-start(bf16[256,512]{1,0:T(8,128)(2,1)} %project.13), channel_id=1, source_target_pairs={{0,2},{1,3},{2,0},{3,1},{4,6},{5,7},{6,4},{7,5},{8,10},{9,11},{10,... | collective-permute-start | bytes 786440 | tf_op jit(solution)/shard_map/cond/branch_1_fun/ppermute | solution.py:368
  91.4 0.7 copy-start.13

commit v2 on v1

--- a/solution.py
+++ b/solution.py
@@ -313,7 +313,7 @@
 def average_part(rate, new, peer, weights, peer_weights, start, outs):
     rows, model = weights.shape
     columns = new.shape[1]
-    tile = 256
+    tile = 512
     tiles = columns // tile
     hbm = pl.BlockSpec(memory_space=pltpu.HBM)
     shape = jax.ShapeDtypeStruct((rows, model), jnp.bfloat16)

time: 106 us -> 104 us (0.981)
  starting transfers between devices: 18.6 us -> 16.9 us
    ppermute x9, starting transfers between devices: 18.6 us -> 16.9 us  [move(): return lax.ppermute(value, AXES, pairs)]
where the time goes in v2:
time: 104 us; the launch traced here: 103 us
  Pallas kernels  44.4 us (43%)
  waiting for transfers between devices  37.1 us (36%)
  starting transfers between devices  16.9 us (16%)
  local copies, waits for them, and re-layouts  2.79 us (3%)
  between operations  1.45 us (1%)
    ppermute x9, waiting for transfers between devices, move(): return lax.ppermute(value, AXES, pairs)  37.1 us
    ppermute x9, starting transfers between devices, move(): return lax.ppermute(value, AXES, pairs)  16.9 us
    pallas_call x2, Pallas kernels, project(): pl.pallas_call(partial(project_kernel, scale, per), grid=(tiles,), in_spe...  15.9 us
    pallas_call x2, Pallas kernels, moment_part(): pl.pallas_call(partial(moment_kernel, scale, 256), grid_spec=pltpu.Prefet...  12 us
    pallas_call x2, Pallas kernels, average_part(): pl.pallas_call(partial(average_kernel, start), in_specs=[pl.BlockSpec(mem...  6.44 us
    pallas_call x1, Pallas kernels, normalize(): pl.pallas_call(norm_kernel, grid_spec=pltpu.PrefetchScalarGridSpec(num_sc...  4.82 us
    cond x8, local copies, waits for them, and re-layouts  2.79 us
    pallas_call x1, Pallas kernels, pack(): pl.pallas_call(pack_kernel, in_specs=[pl.BlockSpec(memory_space=pltpu.SME...  2.73 us
  transfers between devices with their start and end apart: 9, of which 7 were waited for; matrix products, arithmetic and copies ran while one was open for 0% of the time, Pallas kernels for 40%

profile of v2, /device:TPU:1, one launch (start us, length us, event | category | flops | bytes accessed | tf_op | source)
XLA Modules:
  0.0 103.0 jit_solution(18368945143490052828)
XLA Ops:
  1.3 101.5 %conditional.16 = (bf16[256,1024]{1,0:T(8,128)(2,1)}, bf16[256,4096]{1,0:T(8,128)(2,1)}, bf16[256,4096]{1,0:T(8,128)(2,1)}) conditional(s32[]{:T(128)} %bitcast, (pred[]{:T(512)}, s32[1]{0:T(128)}, bf16[256,4096]{1,0:T(8,128)(2,1)}, f32[1,4096]{1,0:T(1,128)}, bf16[256,1024]{1,0:T(8,128)(2,1)}, ...), branch_computations={%region_0.0_spmd, %region_7.0_spmd, %region_14.0_spmd, %region_21.... | conditional | flops 4305453056 | bytes 154403648 | solution.py:431
  1.5 2.6 %collective-permute-start.33 = (bf16[256,4096]{1,0:T(8,128)(2,1)}, bf16[256,4096]{1,0:T(8,128)(2,1)S(1)}, u32[]{:S(2)}, u32[]{:S(2)}) collective-permute-start(bf16[256,4096]{1,0:T(8,128)(2,1)} %get-tuple-element.481.refs_2_.weights), channel_id=1, source_target_pairs={{0,32},{1,33},{2,34},{3,35},{4,36},{5,37},{6,38},{7,39},{8,40},{9,... | collective-permute-start | bytes 6291464 | tf_op jit(solution)/shard_map/cond/branch_3_fun/ppermute | solution.py:368
  4.1 4.8 %normalize.8 = (bf16[256,2560]{1,0:T(8,128)(2,1)}, bf16[256,2048]{1,0:T(8,128)(2,1)}) custom-call(s32[1]{0:T(128)} %get-tuple-element.475.place, bf16[256,4096]{1,0:T(8,128)(2,1)} %get-tuple-element.476.tok, f32[1,4096]{1,0:T(1,128)} %get-tuple-element.477.gains, bf16[256,1024]{1,0:T(8,128)(2,1)} %get-tuple-element.478.k_far.k_cross, ...), custom_call_target="tpu_custom_call" | custom-call | flops 4194304 | bytes 5242880 | tf_op jit(solution)/shard_map/cond/branch_3_fun/normalize/pallas_call | solution.py:48
  8.9 2.9 %collective-permute-start.32 = (bf16[256,2560]{1,0:T(8,128)(2,1)}, bf16[256,2560]{1,0:T(8,128)(2,1)}, u32[]{:S(2)}, u32[]{:S(2)}) collective-permute-start(bf16[256,2560]{1,0:T(8,128)(2,1)} %get-tuple-element.480), channel_id=1, source_target_pairs={{0,2},{1,3},{2,0},{3,1},{4,6},{5,7},{6,4},{7,5},{8,10},{9,11},{10,... | collective-permute-start | bytes 3932168 | tf_op jit(solution)/shard_map/cond/branch_3_fun/ppermute | solution.py:368
  11.9 21.0 %conditional.9 = ((bf16[256,8448]{1,0:T(8,128)(2,1)}, bf16[256,8448]{1,0:T(8,128)(2,1)}, bf16[256,512]{1,0:T(8,128)(2,1)S(1)})) conditional(s32[]{:T(128)} %convert_element_type.15, () %tuple.133, (s32[1]{0:T(128)}, bf16[256,2560]{1,0:T(8,128)(2,1)}, bf16[256,2048]{1,0:T(8,128)(2,1)}, bf16[256,4096]{1,0:T(8,128)(2,1)}, ...), branch_computations={%region_22.0_spmd, %region_23.0_spmd} | conditional | flops 1073741824 | bytes 49545316 | solution.py:352
  11.9 2.7 %pack.8.refs_0_ = bf16[256,8448]{1,0:T(8,128)(2,1)S(1)} custom-call(s32[1]{0:T(128)} %get-tuple-element.451.place, bf16[256,2560]{1,0:T(8,128)(2,1)} %get-tuple-element.452.refs_0_, bf16[256,2048]{1,0:T(8,128)(2,1)} %get-tuple-element.453.refs_1_, bf16[256,4096]{1,0:T(8,128)(2,1)} %get-tuple-element.454.refs_2_.refs_1_, ...), custom_call_target="tpu_custom_call" | custom-call | bytes 8650752 | tf_op jit(solution)/shard_map/cond/branch_3_fun/cond/branch_1_fun/pack/pallas_call | solution.py:93
  18.2 7.1 %collective-permute-done.28.refs_2_ = bf16[256,8448]{1,0:T(8,128)(2,1)} collective-permute-done((bf16[256,8448]{1,0:T(8,128)(2,1)S(1)}, bf16[256,8448]{1,0:T(8,128)(2,1)}, u32[]{:S(2)}, u32[]{:S(2)}) %collective-permute-start.28) | collective-permute-done | bytes 4325408 | tf_op jit(solution)/shard_map/cond/branch_3_fun/cond/branch_1_fun/ppermute | solution.py:368
  25.3 7.5 %project.16 = bf16[256,512]{1,0:T(8,128)(2,1)S(1)} custom-call(bf16[256,8448]{1,0:T(8,128)(2,1)} %copy-done.9, bf16[256,4096]{1,0:T(8,128)(2,1)} %get-tuple-element.454.refs_2_.refs_1_, bf16[256,8448]{1,0:T(8,128)(2,1)} %collective-permute-done.28.refs_2_), custom_call_target="tpu_custom_call" | custom-call | flops 1073741824 | bytes 6291456 | tf_op jit(solution)/shard_map/cond/branch_3_fun/cond/branch_1_fun/project/pallas_call | solution.py:216
  32.9 7.2 %collective-permute-done.32.refs_0_ = bf16[256,2560]{1,0:T(8,128)(2,1)} collective-permute-done((bf16[256,2560]{1,0:T(8,128)(2,1)}, bf16[256,2560]{1,0:T(8,128)(2,1)}, u32[]{:S(2)}, u32[]{:S(2)}) %collective-permute-start.32) | collective-permute-done | bytes 1310752 | tf_op jit(solution)/shard_map/cond/branch_3_fun/ppermute | solution.py:368
  40.0 12.3 %conditional.10 = ((f32[256,2048]{1,0:T(8,128)}, bf16[256,2048]{1,0:T(8,128)(2,1)}, bf16[256,2560]{1,0:T(8,128)(2,1)})) conditional(s32[]{:T(128)} %convert_element_type.15, () %tuple.132, (bf16[256,2560]{1,0:T(8,128)(2,1)}, s32[1]{0:T(128)}, bf16[256,1024]{1,0:T(8,128)(2,1)S(1)}, bf16[256,8448]{1,0:T(8,128)(2,1)}, bf16[256,8448]{1,0:T(8,128)(2,1)}, ...), branch_computations={%region_24.0_spmd, %region_25.0_spmd} | conditional | flops 1073741824 | bytes 13631560 | solution.py:352
  40.0 3.3 %collective-permute-start.29 = (bf16[256,2560]{1,0:T(8,128)(2,1)}, bf16[256,2560]{1,0:T(8,128)(2,1)}, u32[]{:S(2)}, u32[]{:S(2)}) collective-permute-start(bf16[256,2560]{1,0:T(8,128)(2,1)} %get-tuple-element.459.k_far.n_far), channel_id=1, source_target_pairs={{0,1},{1,0},{2,3},{3,2},{4,5},{5,4},{6,7},{7,6},{8,9},{9,8},{10,11... | collective-permute-start | bytes 3932168 | tf_op jit(solution)/shard_map/cond/branch_3_fun/cond/branch_1_fun/ppermute | solution.py:368
  43.4 3.0 %collective-permute-done.29.k_cross.n_cross = bf16[256,2560]{1,0:T(8,128)(2,1)} collective-permute-done((bf16[256,2560]{1,0:T(8,128)(2,1)}, bf16[256,2560]{1,0:T(8,128)(2,1)}, u32[]{:S(2)}, u32[]{:S(2)}) %collective-permute-start.29) | collective-permute-done | bytes 1310752 | tf_op jit(solution)/shard_map/cond/branch_3_fun/cond/branch_1_fun/ppermute | solution.py:368
  46.4 6.0 %moment_part.16 = (f32[256,2048]{1,0:T(8,128)}, bf16[256,2048]{1,0:T(8,128)(2,1)}) custom-call(s32[1]{0:T(128)} %get-tuple-element.456.place, bf16[256,1024]{1,0:T(8,128)(2,1)S(1)} %get-tuple-element.457.k_own, bf16[256,8448]{1,0:T(8,128)(2,1)} %get-tuple-element.458.k_sib.n_sib, bf16[256,2560]{1,0:T(8,128)(2,1)} %get-tuple-element.459.k_far.n_far, ...), custom_call_target="tpu_custom_call" | custom-call | flops 1073741824 | bytes 8388608 | tf_op jit(solution)/shard_map/cond/branch_3_fun/cond/branch_1_fun/moment_part/pallas_call | solution.py:144
  54.0 8.5 %collective-permute-done.31.refs_1_ = bf16[256,2048]{1,0:T(8,128)(2,1)} collective-permute-done((bf16[256,2048]{1,0:T(8,128)(2,1)}, bf16[256,2048]{1,0:T(8,128)(2,1)}, u32[]{:S(2)}, u32[]{:S(2)}) %collective-permute-start.31) | collective-permute-done | bytes 1048608 | tf_op jit(solution)/shard_map/cond/branch_3_fun/ppermute | solution.py:368
  62.5 10.5 %conditional.11 = ((f32[256,2048]{1,0:T(8,128)}, bf16[256,2048]{1,0:T(8,128)(2,1)})) conditional(s32[]{:T(128)} %convert_element_type.15, () %tuple.131, (bf16[256,2048]{1,0:T(8,128)(2,1)}, s32[1]{0:T(128)}, bf16[256,1024]{1,0:T(8,128)(2,1)S(1)}, bf16[256,8448]{1,0:T(8,128)(2,1)}, bf16[256,2560]{1,0:T(8,128)(2,1)}, ...), branch_computations={%region_26.0_spmd, %region_27.0_spmd} | conditional | flops 1073741824 | bytes 12582960 | solution.py:352
  64.4 2.6 %collective-permute-done.30.n_cross = bf16[256,2048]{1,0:T(8,128)(2,1)} collective-permute-done((bf16[256,2048]{1,0:T(8,128)(2,1)}, bf16[256,2048]{1,0:T(8,128)(2,1)}, u32[]{:S(2)}, u32[]{:S(2)}) %collective-permute-start.30) | collective-permute-done | bytes 1048608 | tf_op jit(solution)/shard_map/cond/branch_3_fun/cond/branch_1_fun/ppermute | solution.py:368
  67.0 6.0 %moment_part.17 = (f32[256,2048]{1,0:T(8,128)}, bf16[256,2048]{1,0:T(8,128)(2,1)}) custom-call(s32[1]{0:T(128)} %get-tuple-element.466.place, bf16[256,1024]{1,0:T(8,128)(2,1)S(1)} %get-tuple-element.467.k_own, bf16[256,8448]{1,0:T(8,128)(2,1)} %get-tuple-element.468.k_sib.n_sib, bf16[256,2560]{1,0:T(8,128)(2,1)} %get-tuple-element.469.k_far, ...), custom_call_target="tpu_custom_call" | custom-call | flops 1073741824 | bytes 8388608 | tf_op jit(solution)/shard_map/cond/branch_3_fun/cond/branch_1_fun/moment_part/pallas_call | solution.py:144
  73.1 8.4 %project.17 = bf16[256,512]{1,0:T(8,128)(2,1)} custom-call(bf16[256,2560]{1,0:T(8,128)(2,1)} %collective-permute-done.32.refs_0_, bf16[256,2048]{1,0:T(8,128)(2,1)} %collective-permute-done.31.refs_1_, bf16[256,4096]{1,0:T(8,128)(2,1)} %get-tuple-element.481.refs_2_.weights, bf16[256,8448]{1,0:T(8,128)(2,1)} %get-tuple-element.484.refs_3_), custom_call_target="tpu_custom_call" | custom-call | flops 1073741824 | bytes 6291456 | tf_op jit(solution)/shard_map/cond/branch_3_fun/project/pallas_call | solution.py:216
  81.5 2.9 %collective-permute-start.36 = (bf16[256,512]{1,0:T(8,128)(2,1)}, bf16[256,512]{1,0:T(8,128)(2,1)S(1)}, u32[]{:S(2)}, u32[]{:S(2)}) collective-permute-start(bf16[256,512]{1,0:T(8,128)(2,1)} %project.17), channel_id=1, source_target_pairs={{0,2},{1,3},{2,0},{3,1},{4,6},{5,7},{6,4},{7,5},{8,10},{9,11},{10,... | collective-permute-start | bytes 786440 | tf_op jit(solution)/shard_map/cond/branch_3_fun/ppermute | solution.py:368
  84.4 3.4 %average_part.16 = (bf16[256,4096]{1,0:T(8,128)(2,1)}, bf16[256,4096]{1,0:T(8,128)(2,1)}) custom-call(f32[1]{0:T(128)} %get-tuple-element.495.rate, f32[256,2048]{1,0:T(8,128)} %get-tuple-element.496.new, bf16[256,2048]{1,0:T(8,128)(2,1)} %collective-permute-done.35.peer, bf16[256,4096]{1,0:T(8,128)(2,1)} %get-tuple-element.481.refs_2_.weights, ...), custom_call_target="tpu_custom_call" | custom-call | flops 3145728 | bytes 7340032 | tf_op jit(solution)/shard_map/cond/branch_3_fun/average_part/pallas_call | solution.py:321
  87.8 2.6 %collective-permute-done.36.refs_2_.refs_3_ = bf16[256,512]{1,0:T(8,128)(2,1)S(1)} collective-permute-done((bf16[256,512]{1,0:T(8,128)(2,1)}, bf16[256,512]{1,0:T(8,128)(2,1)S(1)}, u32[]{:S(2)}, u32[]{:S(2)}) %collective-permute-start.36) | collective-permute-done | bytes 262176 | tf_op jit(solution)/shard_map/cond/branch_3_fun/ppermute | solution.py:368
  91.1 2.6 %place_blocks.8 = bf16[256,1024]{1,0:T(8,128)(2,1)} custom-call(s32[1]{0:T(128)} %get-tuple-element.475.place, bf16[256,512]{1,0:T(8,128)(2,1)} %copy-done.19, bf16[256,512]{1,0:T(8,128)(2,1)} %copy-done.19, bf16[256,512]{1,0:T(8,128)(2,1)} %copy-done.15, bf16[256,512]{1,0:T(8,128)(2,1)} %copy-done.15), custom_call_target="tpu_custom_call" | custom-call | bytes 1048576 | tf_op jit(solution)/shard_map/cond/branch_3_fun/place_blocks/pallas_call | solution.py:249
  93.7 6.1 %collective-permute-done.34.peer = bf16[256,2048]{1,0:T(8,128)(2,1)S(1)} collective-permute-done((bf16[256,2048]{1,0:T(8,128)(2,1)}, bf16[256,2048]{1,0:T(8,128)(2,1)S(1)}, u32[]{:S(2)}, u32[]{:S(2)}) %collective-permute-start.34) | collective-permute-done | bytes 1048608 | tf_op jit(solution)/shard_map/cond/branch_3_fun/ppermute | solution.py:368
  99.7 3.1 %average_part.17 = (bf16[256,4096]{1,0:T(8,128)(2,1)}, bf16[256,4096]{1,0:T(8,128)(2,1)}) custom-call(f32[1]{0:T(128)} %get-tuple-element.495.rate, f32[256,2048]{1,0:T(8,128)} %get-tuple-element.503.new, bf16[256,2048]{1,0:T(8,128)(2,1)S(1)} %collective-permute-done.34.peer, ...), custom_call_target="tpu_custom_call", output_to_operand_aliasing={{0}: (5, {}), {1}: (6, {})} | custom-call | flops 3145728 | bytes 7340032 | tf_op jit(solution)/shard_map/cond/branch_3_fun/average_part/pallas_call | solution.py:321
  (15 shorter events, 8.0 us)
Async XLA Ops:
  1.5 10.4 %copy-start.4 = (bf16[256,1024]{1,0:T(8,128)(2,1)S(1)}, bf16[256,1024]{1,0:T(8,128)(2,1)}, u32[]{:S(2)}) copy-start(bf16[256,1024]{1,0:T(8,128)(2,1)} %get-tuple-element.478.k_far.k_cross) | copy-start | bytes 1572868 | tf_op jit(solution)/shard_map/cond
  1.5 50.8 %collective-permute-start.33 = (bf16[256,4096]{1,0:T(8,128)(2,1)}, bf16[256,4096]{1,0:T(8,128)(2,1)S(1)}, u32[]{:S(2)}, u32[]{:S(2)}) collective-permute-start(bf16[256,4096]{1,0:T(8,128)(2,1)} %get-tuple-element.481.refs_2_.weights), channel_id=1, source_target_pairs={{0,32},{1,33},{2,34},{3,35},{4,36},{5,37},{6,38},{7,39},{8,40},{9,... | collective-permute-start | bytes 6291464 | tf_op jit(solution)/shard_map/cond/branch_3_fun/ppermute | solution.py:368
  8.9 31.1 %collective-permute-start.32 = (bf16[256,2560]{1,0:T(8,128)(2,1)}, bf16[256,2560]{1,0:T(8,128)(2,1)}, u32[]{:S(2)}, u32[]{:S(2)}) collective-permute-start(bf16[256,2560]{1,0:T(8,128)(2,1)} %get-tuple-element.480), channel_id=1, source_target_pairs={{0,2},{1,3},{2,0},{3,1},{4,6},{5,7},{6,4},{7,5},{8,10},{9,11},{10,... | collective-permute-start | bytes 3932168 | tf_op jit(solution)/shard_map/cond/branch_3_fun/ppermute | solution.py:368
  11.8 50.7 %collective-permute-start.31 = (bf16[256,2048]{1,0:T(8,128)(2,1)}, bf16[256,2048]{1,0:T(8,128)(2,1)}, u32[]{:S(2)}, u32[]{:S(2)}) collective-permute-start(bf16[256,2048]{1,0:T(8,128)(2,1)} %get-tuple-element.479), channel_id=1, source_target_pairs={{0,2},{1,3},{2,0},{3,1},{4,6},{5,7},{6,4},{7,5},{8,10},{9,11},{10,... | collective-permute-start | bytes 3145736 | tf_op jit(solution)/shard_map/cond/branch_3_fun/ppermute | solution.py:368
  14.6 2.1 %copy-start.9 = (bf16[256,8448]{1,0:T(8,128)(2,1)}, bf16[256,8448]{1,0:T(8,128)(2,1)S(1)}, u32[]{:S(2)}) copy-start(bf16[256,8448]{1,0:T(8,128)(2,1)S(1)} %pack.8.refs_0_) | copy-start | bytes 12976132 | tf_op jit(solution)/shard_map/cond/branch_3_fun/cond
  16.7 8.6 %collective-permute-start.28 = (bf16[256,8448]{1,0:T(8,128)(2,1)S(1)}, bf16[256,8448]{1,0:T(8,128)(2,1)}, u32[]{:S(2)}, u32[]{:S(2)}) collective-permute-start(bf16[256,8448]{1,0:T(8,128)(2,1)S(1)} %pack.8.refs_0_), channel_id=1, source_target_pairs={{0,1},{1,0},{2,3},{3,2},{4,5},{5,4},{6,7},{7,6},{8,9},{9,8},{10,11... | collective-permute-start | bytes 12976136 | tf_op jit(solution)/shard_map/cond/branch_3_fun/cond/branch_1_fun/ppermute | solution.py:368
  32.9 7.2 %copy-start.19 = (bf16[256,512]{1,0:T(8,128)(2,1)}, bf16[256,512]{1,0:T(8,128)(2,1)S(1)}, u32[]{:S(2)}) copy-start(bf16[256,512]{1,0:T(8,128)(2,1)S(1)} %get-tuple-element.492.refs_0_.refs_1_) | copy-start | bytes 786436 | tf_op jit(solution)/shard_map/cond
  40.0 6.3 %collective-permute-start.29 = (bf16[256,2560]{1,0:T(8,128)(2,1)}, bf16[256,2560]{1,0:T(8,128)(2,1)}, u32[]{:S(2)}, u32[]{:S(2)}) collective-permute-start(bf16[256,2560]{1,0:T(8,128)(2,1)} %get-tuple-element.459.k_far.n_far), channel_id=1, source_target_pairs={{0,1},{1,0},{2,3},{3,2},{4,5},{5,4},{6,7},{7,6},{8,9},{9,8},{10,11... | collective-permute-start | bytes 3932168 | tf_op jit(solution)/shard_map/cond/branch_3_fun/cond/branch_1_fun/ppermute | solution.py:368
  52.3 29.1 %collective-permute-start.35 = (bf16[256,2048]{1,0:T(8,128)(2,1)}, bf16[256,2048]{1,0:T(8,128)(2,1)}, u32[]{:S(2)}, u32[]{:S(2)}) collective-permute-start(bf16[256,2048]{1,0:T(8,128)(2,1)} %get-tuple-element.488), channel_id=1, source_target_pairs={{0,32},{1,33},{2,34},{3,35},{4,36},{5,37},{6,38},{7,39},{8,40},{9,... | collective-permute-start | bytes 3145736 | tf_op jit(solution)/shard_map/cond/branch_3_fun/ppermute | solution.py:368
  62.5 4.5 %collective-permute-start.30 = (bf16[256,2048]{1,0:T(8,128)(2,1)}, bf16[256,2048]{1,0:T(8,128)(2,1)}, u32[]{:S(2)}, u32[]{:S(2)}) collective-permute-start(bf16[256,2048]{1,0:T(8,128)(2,1)} %get-tuple-element.472.n_far), channel_id=1, source_target_pairs={{0,1},{1,0},{2,3},{3,2},{4,5},{5,4},{6,7},{7,6},{8,9},{9,8},{10,11... | collective-permute-start | bytes 3145736 | tf_op jit(solution)/shard_map/cond/branch_3_fun/cond/branch_1_fun/ppermute | solution.py:368
  73.0 26.7 %collective-permute-start.34 = (bf16[256,2048]{1,0:T(8,128)(2,1)}, bf16[256,2048]{1,0:T(8,128)(2,1)S(1)}, u32[]{:S(2)}, u32[]{:S(2)}) collective-permute-start(bf16[256,2048]{1,0:T(8,128)(2,1)} %get-tuple-element.491), channel_id=1, source_target_pairs={{0,32},{1,33},{2,34},{3,35},{4,36},{5,37},{6,38},{7,39},{8,40},{9,... | collective-permute-start | bytes 3145736 | tf_op jit(solution)/shard_map/cond/branch_3_fun/ppermute | solution.py:368
  81.5 8.9 %collective-permute-start.36 = (bf16[256,512]{1,0:T(8,128)(2,1)}, bf16[256,512]{1,0:T(8,128)(2,1)S(1)}, u32[]{:S(2)}, u32[]{:S(2)}) collective-permute-start(bf16[256,512]{1,0:T(8,128)(2,1)} %project.17), channel_id=1, source_target_pairs={{0,2},{1,3},{2,0},{3,1},{4,6},{5,7},{6,4},{7,5},{8,10},{9,11},{10,... | collective-permute-start | bytes 786440 | tf_op jit(solution)/shard_map/cond/branch_3_fun/ppermute | solution.py:368
  90.4 0.7 copy-start.15

commit v3 on v2

--- a/solution.py
+++ b/solution.py
@@ -265,7 +265,7 @@
 def average_kernel(start, rate, new, peer, weights, peer_weights, *refs):
     weight_out, moment_out, n_buf, p_buf, w_buf, q_buf, wo_buf, mo_buf, in_sems, out_sems = refs[-10:]
     tiles, rows, tile = n_buf.shape
-    step = 64
+    step = 128
 
     def columns(t, start):
         return pl.ds(pl.multiple_of(start + t * tile, tile), tile)

time: 104 us -> 104 us (level)
  no operation moved by 1% of the time
where the time goes in v3:
time: 104 us; the launch traced here: 103 us
  Pallas kernels  44.4 us (43%)
  waiting for transfers between devices  37.1 us (36%)
  starting transfers between devices  16.9 us (16%)
  local copies, waits for them, and re-layouts  2.79 us (3%)
  between operations  1.45 us (1%)
    ppermute x9, waiting for transfers between devices, move(): return lax.ppermute(value, AXES, pairs)  37.1 us
    ppermute x9, starting transfers between devices, move(): return lax.ppermute(value, AXES, pairs)  16.9 us
    pallas_call x2, Pallas kernels, project(): pl.pallas_call(partial(project_kernel, scale, per), grid=(tiles,), in_spe...  15.9 us
    pallas_call x2, Pallas kernels, moment_part(): pl.pallas_call(partial(moment_kernel, scale, 256), grid_spec=pltpu.Prefet...  12 us
    pallas_call x2, Pallas kernels, average_part(): pl.pallas_call(partial(average_kernel, start), in_specs=[pl.BlockSpec(mem...  6.42 us
    pallas_call x1, Pallas kernels, normalize(): pl.pallas_call(norm_kernel, grid_spec=pltpu.PrefetchScalarGridSpec(num_sc...  4.82 us
    cond x8, local copies, waits for them, and re-layouts  2.79 us
    pallas_call x1, Pallas kernels, pack(): pl.pallas_call(pack_kernel, in_specs=[pl.BlockSpec(memory_space=pltpu.SME...  2.73 us
  transfers between devices with their start and end apart: 9, of which 7 were waited for; matrix products, arithmetic and copies ran while one was open for 0% of the time, Pallas kernels for 40%

profile of v3, /device:TPU:1, one launch (start us, length us, event | category | flops | bytes accessed | tf_op | source)
XLA Modules:
  0.0 103.0 jit_solution(11898976331876622612)
XLA Ops:
  1.3 101.5 %conditional.16 = (bf16[256,1024]{1,0:T(8,128)(2,1)}, bf16[256,4096]{1,0:T(8,128)(2,1)}, bf16[256,4096]{1,0:T(8,128)(2,1)}) conditional(s32[]{:T(128)} %bitcast, (pred[]{:T(512)}, s32[1]{0:T(128)}, bf16[256,4096]{1,0:T(8,128)(2,1)}, f32[1,4096]{1,0:T(1,128)}, bf16[256,1024]{1,0:T(8,128)(2,1)}, ...), branch_computations={%region_0.0_spmd, %region_7.0_spmd, %region_14.0_spmd, %region_21.... | conditional | flops 4305453056 | bytes 154403648 | solution.py:431
  1.5 2.6 %collective-permute-start.33 = (bf16[256,4096]{1,0:T(8,128)(2,1)}, bf16[256,4096]{1,0:T(8,128)(2,1)S(1)}, u32[]{:S(2)}, u32[]{:S(2)}) collective-permute-start(bf16[256,4096]{1,0:T(8,128)(2,1)} %get-tuple-element.481.refs_2_.weights), channel_id=1, source_target_pairs={{0,32},{1,33},{2,34},{3,35},{4,36},{5,37},{6,38},{7,39},{8,40},{9,... | collective-permute-start | bytes 6291464 | tf_op jit(solution)/shard_map/cond/branch_3_fun/ppermute | solution.py:368
  4.1 4.8 %normalize.8 = (bf16[256,2560]{1,0:T(8,128)(2,1)}, bf16[256,2048]{1,0:T(8,128)(2,1)}) custom-call(s32[1]{0:T(128)} %get-tuple-element.475.place, bf16[256,4096]{1,0:T(8,128)(2,1)} %get-tuple-element.476.tok, f32[1,4096]{1,0:T(1,128)} %get-tuple-element.477.gains, bf16[256,1024]{1,0:T(8,128)(2,1)} %get-tuple-element.478.k_far.k_cross, ...), custom_call_target="tpu_custom_call" | custom-call | flops 4194304 | bytes 5242880 | tf_op jit(solution)/shard_map/cond/branch_3_fun/normalize/pallas_call | solution.py:48
  8.9 2.9 %collective-permute-start.32 = (bf16[256,2560]{1,0:T(8,128)(2,1)}, bf16[256,2560]{1,0:T(8,128)(2,1)}, u32[]{:S(2)}, u32[]{:S(2)}) collective-permute-start(bf16[256,2560]{1,0:T(8,128)(2,1)} %get-tuple-element.480), channel_id=1, source_target_pairs={{0,2},{1,3},{2,0},{3,1},{4,6},{5,7},{6,4},{7,5},{8,10},{9,11},{10,... | collective-permute-start | bytes 3932168 | tf_op jit(solution)/shard_map/cond/branch_3_fun/ppermute | solution.py:368
  11.9 21.0 %conditional.9 = ((bf16[256,8448]{1,0:T(8,128)(2,1)}, bf16[256,8448]{1,0:T(8,128)(2,1)}, bf16[256,512]{1,0:T(8,128)(2,1)S(1)})) conditional(s32[]{:T(128)} %convert_element_type.15, () %tuple.133, (s32[1]{0:T(128)}, bf16[256,2560]{1,0:T(8,128)(2,1)}, bf16[256,2048]{1,0:T(8,128)(2,1)}, bf16[256,4096]{1,0:T(8,128)(2,1)}, ...), branch_computations={%region_22.0_spmd, %region_23.0_spmd} | conditional | flops 1073741824 | bytes 49545316 | solution.py:352
  11.9 2.7 %pack.8.refs_0_ = bf16[256,8448]{1,0:T(8,128)(2,1)S(1)} custom-call(s32[1]{0:T(128)} %get-tuple-element.451.place, bf16[256,2560]{1,0:T(8,128)(2,1)} %get-tuple-element.452.refs_0_, bf16[256,2048]{1,0:T(8,128)(2,1)} %get-tuple-element.453.refs_1_, bf16[256,4096]{1,0:T(8,128)(2,1)} %get-tuple-element.454.refs_2_.refs_1_, ...), custom_call_target="tpu_custom_call" | custom-call | bytes 8650752 | tf_op jit(solution)/shard_map/cond/branch_3_fun/cond/branch_1_fun/pack/pallas_call | solution.py:93
  18.2 7.1 %collective-permute-done.28.refs_2_ = bf16[256,8448]{1,0:T(8,128)(2,1)} collective-permute-done((bf16[256,8448]{1,0:T(8,128)(2,1)S(1)}, bf16[256,8448]{1,0:T(8,128)(2,1)}, u32[]{:S(2)}, u32[]{:S(2)}) %collective-permute-start.28) | collective-permute-done | bytes 4325408 | tf_op jit(solution)/shard_map/cond/branch_3_fun/cond/branch_1_fun/ppermute | solution.py:368
  25.3 7.5 %project.16 = bf16[256,512]{1,0:T(8,128)(2,1)S(1)} custom-call(bf16[256,8448]{1,0:T(8,128)(2,1)} %copy-done.9, bf16[256,4096]{1,0:T(8,128)(2,1)} %get-tuple-element.454.refs_2_.refs_1_, bf16[256,8448]{1,0:T(8,128)(2,1)} %collective-permute-done.28.refs_2_), custom_call_target="tpu_custom_call" | custom-call | flops 1073741824 | bytes 6291456 | tf_op jit(solution)/shard_map/cond/branch_3_fun/cond/branch_1_fun/project/pallas_call | solution.py:216
  32.9 7.2 %collective-permute-done.32.refs_0_ = bf16[256,2560]{1,0:T(8,128)(2,1)} collective-permute-done((bf16[256,2560]{1,0:T(8,128)(2,1)}, bf16[256,2560]{1,0:T(8,128)(2,1)}, u32[]{:S(2)}, u32[]{:S(2)}) %collective-permute-start.32) | collective-permute-done | bytes 1310752 | tf_op jit(solution)/shard_map/cond/branch_3_fun/ppermute | solution.py:368
  40.0 12.3 %conditional.10 = ((f32[256,2048]{1,0:T(8,128)}, bf16[256,2048]{1,0:T(8,128)(2,1)}, bf16[256,2560]{1,0:T(8,128)(2,1)})) conditional(s32[]{:T(128)} %convert_element_type.15, () %tuple.132, (bf16[256,2560]{1,0:T(8,128)(2,1)}, s32[1]{0:T(128)}, bf16[256,1024]{1,0:T(8,128)(2,1)S(1)}, bf16[256,8448]{1,0:T(8,128)(2,1)}, bf16[256,8448]{1,0:T(8,128)(2,1)}, ...), branch_computations={%region_24.0_spmd, %region_25.0_spmd} | conditional | flops 1073741824 | bytes 13631560 | solution.py:352
  40.0 3.3 %collective-permute-start.29 = (bf16[256,2560]{1,0:T(8,128)(2,1)}, bf16[256,2560]{1,0:T(8,128)(2,1)}, u32[]{:S(2)}, u32[]{:S(2)}) collective-permute-start(bf16[256,2560]{1,0:T(8,128)(2,1)} %get-tuple-element.459.k_far.n_far), channel_id=1, source_target_pairs={{0,1},{1,0},{2,3},{3,2},{4,5},{5,4},{6,7},{7,6},{8,9},{9,8},{10,11... | collective-permute-start | bytes 3932168 | tf_op jit(solution)/shard_map/cond/branch_3_fun/cond/branch_1_fun/ppermute | solution.py:368
  43.4 3.0 %collective-permute-done.29.k_cross.n_cross = bf16[256,2560]{1,0:T(8,128)(2,1)} collective-permute-done((bf16[256,2560]{1,0:T(8,128)(2,1)}, bf16[256,2560]{1,0:T(8,128)(2,1)}, u32[]{:S(2)}, u32[]{:S(2)}) %collective-permute-start.29) | collective-permute-done | bytes 1310752 | tf_op jit(solution)/shard_map/cond/branch_3_fun/cond/branch_1_fun/ppermute | solution.py:368
  46.4 6.0 %moment_part.16 = (f32[256,2048]{1,0:T(8,128)}, bf16[256,2048]{1,0:T(8,128)(2,1)}) custom-call(s32[1]{0:T(128)} %get-tuple-element.456.place, bf16[256,1024]{1,0:T(8,128)(2,1)S(1)} %get-tuple-element.457.k_own, bf16[256,8448]{1,0:T(8,128)(2,1)} %get-tuple-element.458.k_sib.n_sib, bf16[256,2560]{1,0:T(8,128)(2,1)} %get-tuple-element.459.k_far.n_far, ...), custom_call_target="tpu_custom_call" | custom-call | flops 1073741824 | bytes 8388608 | tf_op jit(solution)/shard_map/cond/branch_3_fun/cond/branch_1_fun/moment_part/pallas_call | solution.py:144
  54.0 8.5 %collective-permute-done.31.refs_1_ = bf16[256,2048]{1,0:T(8,128)(2,1)} collective-permute-done((bf16[256,2048]{1,0:T(8,128)(2,1)}, bf16[256,2048]{1,0:T(8,128)(2,1)}, u32[]{:S(2)}, u32[]{:S(2)}) %collective-permute-start.31) | collective-permute-done | bytes 1048608 | tf_op jit(solution)/shard_map/cond/branch_3_fun/ppermute | solution.py:368
  62.5 10.5 %conditional.11 = ((f32[256,2048]{1,0:T(8,128)}, bf16[256,2048]{1,0:T(8,128)(2,1)})) conditional(s32[]{:T(128)} %convert_element_type.15, () %tuple.131, (bf16[256,2048]{1,0:T(8,128)(2,1)}, s32[1]{0:T(128)}, bf16[256,1024]{1,0:T(8,128)(2,1)S(1)}, bf16[256,8448]{1,0:T(8,128)(2,1)}, bf16[256,2560]{1,0:T(8,128)(2,1)}, ...), branch_computations={%region_26.0_spmd, %region_27.0_spmd} | conditional | flops 1073741824 | bytes 12582960 | solution.py:352
  64.4 2.6 %collective-permute-done.30.n_cross = bf16[256,2048]{1,0:T(8,128)(2,1)} collective-permute-done((bf16[256,2048]{1,0:T(8,128)(2,1)}, bf16[256,2048]{1,0:T(8,128)(2,1)}, u32[]{:S(2)}, u32[]{:S(2)}) %collective-permute-start.30) | collective-permute-done | bytes 1048608 | tf_op jit(solution)/shard_map/cond/branch_3_fun/cond/branch_1_fun/ppermute | solution.py:368
  67.0 6.0 %moment_part.17 = (f32[256,2048]{1,0:T(8,128)}, bf16[256,2048]{1,0:T(8,128)(2,1)}) custom-call(s32[1]{0:T(128)} %get-tuple-element.466.place, bf16[256,1024]{1,0:T(8,128)(2,1)S(1)} %get-tuple-element.467.k_own, bf16[256,8448]{1,0:T(8,128)(2,1)} %get-tuple-element.468.k_sib.n_sib, bf16[256,2560]{1,0:T(8,128)(2,1)} %get-tuple-element.469.k_far, ...), custom_call_target="tpu_custom_call" | custom-call | flops 1073741824 | bytes 8388608 | tf_op jit(solution)/shard_map/cond/branch_3_fun/cond/branch_1_fun/moment_part/pallas_call | solution.py:144
  73.1 8.4 %project.17 = bf16[256,512]{1,0:T(8,128)(2,1)} custom-call(bf16[256,2560]{1,0:T(8,128)(2,1)} %collective-permute-done.32.refs_0_, bf16[256,2048]{1,0:T(8,128)(2,1)} %collective-permute-done.31.refs_1_, bf16[256,4096]{1,0:T(8,128)(2,1)} %get-tuple-element.481.refs_2_.weights, bf16[256,8448]{1,0:T(8,128)(2,1)} %get-tuple-element.484.refs_3_), custom_call_target="tpu_custom_call" | custom-call | flops 1073741824 | bytes 6291456 | tf_op jit(solution)/shard_map/cond/branch_3_fun/project/pallas_call | solution.py:216
  81.5 2.9 %collective-permute-start.36 = (bf16[256,512]{1,0:T(8,128)(2,1)}, bf16[256,512]{1,0:T(8,128)(2,1)S(1)}, u32[]{:S(2)}, u32[]{:S(2)}) collective-permute-start(bf16[256,512]{1,0:T(8,128)(2,1)} %project.17), channel_id=1, source_target_pairs={{0,2},{1,3},{2,0},{3,1},{4,6},{5,7},{6,4},{7,5},{8,10},{9,11},{10,... | collective-permute-start | bytes 786440 | tf_op jit(solution)/shard_map/cond/branch_3_fun/ppermute | solution.py:368
  84.4 3.4 %average_part.16 = (bf16[256,4096]{1,0:T(8,128)(2,1)}, bf16[256,4096]{1,0:T(8,128)(2,1)}) custom-call(f32[1]{0:T(128)} %get-tuple-element.495.rate, f32[256,2048]{1,0:T(8,128)} %get-tuple-element.496.new, bf16[256,2048]{1,0:T(8,128)(2,1)} %collective-permute-done.35.peer, bf16[256,4096]{1,0:T(8,128)(2,1)} %get-tuple-element.481.refs_2_.weights, ...), custom_call_target="tpu_custom_call" | custom-call | flops 3145728 | bytes 7340032 | tf_op jit(solution)/shard_map/cond/branch_3_fun/average_part/pallas_call | solution.py:321
  87.8 2.6 %collective-permute-done.36.refs_2_.refs_3_ = bf16[256,512]{1,0:T(8,128)(2,1)S(1)} collective-permute-done((bf16[256,512]{1,0:T(8,128)(2,1)}, bf16[256,512]{1,0:T(8,128)(2,1)S(1)}, u32[]{:S(2)}, u32[]{:S(2)}) %collective-permute-start.36) | collective-permute-done | bytes 262176 | tf_op jit(solution)/shard_map/cond/branch_3_fun/ppermute | solution.py:368
  91.1 2.6 %place_blocks.8 = bf16[256,1024]{1,0:T(8,128)(2,1)} custom-call(s32[1]{0:T(128)} %get-tuple-element.475.place, bf16[256,512]{1,0:T(8,128)(2,1)} %copy-done.19, bf16[256,512]{1,0:T(8,128)(2,1)} %copy-done.19, bf16[256,512]{1,0:T(8,128)(2,1)} %copy-done.15, bf16[256,512]{1,0:T(8,128)(2,1)} %copy-done.15), custom_call_target="tpu_custom_call" | custom-call | bytes 1048576 | tf_op jit(solution)/shard_map/cond/branch_3_fun/place_blocks/pallas_call | solution.py:249
  93.7 6.1 %collective-permute-done.34.peer = bf16[256,2048]{1,0:T(8,128)(2,1)S(1)} collective-permute-done((bf16[256,2048]{1,0:T(8,128)(2,1)}, bf16[256,2048]{1,0:T(8,128)(2,1)S(1)}, u32[]{:S(2)}, u32[]{:S(2)}) %collective-permute-start.34) | collective-permute-done | bytes 1048608 | tf_op jit(solution)/shard_map/cond/branch_3_fun/ppermute | solution.py:368
  99.7 3.1 %average_part.17 = (bf16[256,4096]{1,0:T(8,128)(2,1)}, bf16[256,4096]{1,0:T(8,128)(2,1)}) custom-call(f32[1]{0:T(128)} %get-tuple-element.495.rate, f32[256,2048]{1,0:T(8,128)} %get-tuple-element.503.new, bf16[256,2048]{1,0:T(8,128)(2,1)S(1)} %collective-permute-done.34.peer, ...), custom_call_target="tpu_custom_call", output_to_operand_aliasing={{0}: (5, {}), {1}: (6, {})} | custom-call | flops 3145728 | bytes 7340032 | tf_op jit(solution)/shard_map/cond/branch_3_fun/average_part/pallas_call | solution.py:321
  (15 shorter events, 8.0 us)
Async XLA Ops:
  1.5 10.4 %copy-start.4 = (bf16[256,1024]{1,0:T(8,128)(2,1)S(1)}, bf16[256,1024]{1,0:T(8,128)(2,1)}, u32[]{:S(2)}) copy-start(bf16[256,1024]{1,0:T(8,128)(2,1)} %get-tuple-element.478.k_far.k_cross) | copy-start | bytes 1572868 | tf_op jit(solution)/shard_map/cond
  1.5 50.8 %collective-permute-start.33 = (bf16[256,4096]{1,0:T(8,128)(2,1)}, bf16[256,4096]{1,0:T(8,128)(2,1)S(1)}, u32[]{:S(2)}, u32[]{:S(2)}) collective-permute-start(bf16[256,4096]{1,0:T(8,128)(2,1)} %get-tuple-element.481.refs_2_.weights), channel_id=1, source_target_pairs={{0,32},{1,33},{2,34},{3,35},{4,36},{5,37},{6,38},{7,39},{8,40},{9,... | collective-permute-start | bytes 6291464 | tf_op jit(solution)/shard_map/cond/branch_3_fun/ppermute | solution.py:368
  8.9 31.1 %collective-permute-start.32 = (bf16[256,2560]{1,0:T(8,128)(2,1)}, bf16[256,2560]{1,0:T(8,128)(2,1)}, u32[]{:S(2)}, u32[]{:S(2)}) collective-permute-start(bf16[256,2560]{1,0:T(8,128)(2,1)} %get-tuple-element.480), channel_id=1, source_target_pairs={{0,2},{1,3},{2,0},{3,1},{4,6},{5,7},{6,4},{7,5},{8,10},{9,11},{10,... | collective-permute-start | bytes 3932168 | tf_op jit(solution)/shard_map/cond/branch_3_fun/ppermute | solution.py:368
  11.8 50.7 %collective-permute-start.31 = (bf16[256,2048]{1,0:T(8,128)(2,1)}, bf16[256,2048]{1,0:T(8,128)(2,1)}, u32[]{:S(2)}, u32[]{:S(2)}) collective-permute-start(bf16[256,2048]{1,0:T(8,128)(2,1)} %get-tuple-element.479), channel_id=1, source_target_pairs={{0,2},{1,3},{2,0},{3,1},{4,6},{5,7},{6,4},{7,5},{8,10},{9,11},{10,... | collective-permute-start | bytes 3145736 | tf_op jit(solution)/shard_map/cond/branch_3_fun/ppermute | solution.py:368
  14.6 2.1 %copy-start.9 = (bf16[256,8448]{1,0:T(8,128)(2,1)}, bf16[256,8448]{1,0:T(8,128)(2,1)S(1)}, u32[]{:S(2)}) copy-start(bf16[256,8448]{1,0:T(8,128)(2,1)S(1)} %pack.8.refs_0_) | copy-start | bytes 12976132 | tf_op jit(solution)/shard_map/cond/branch_3_fun/cond
  16.7 8.6 %collective-permute-start.28 = (bf16[256,8448]{1,0:T(8,128)(2,1)S(1)}, bf16[256,8448]{1,0:T(8,128)(2,1)}, u32[]{:S(2)}, u32[]{:S(2)}) collective-permute-start(bf16[256,8448]{1,0:T(8,128)(2,1)S(1)} %pack.8.refs_0_), channel_id=1, source_target_pairs={{0,1},{1,0},{2,3},{3,2},{4,5},{5,4},{6,7},{7,6},{8,9},{9,8},{10,11... | collective-permute-start | bytes 12976136 | tf_op jit(solution)/shard_map/cond/branch_3_fun/cond/branch_1_fun/ppermute | solution.py:368
  32.9 7.2 %copy-start.19 = (bf16[256,512]{1,0:T(8,128)(2,1)}, bf16[256,512]{1,0:T(8,128)(2,1)S(1)}, u32[]{:S(2)}) copy-start(bf16[256,512]{1,0:T(8,128)(2,1)S(1)} %get-tuple-element.492.refs_0_.refs_1_) | copy-start | bytes 786436 | tf_op jit(solution)/shard_map/cond
  40.0 6.3 %collective-permute-start.29 = (bf16[256,2560]{1,0:T(8,128)(2,1)}, bf16[256,2560]{1,0:T(8,128)(2,1)}, u32[]{:S(2)}, u32[]{:S(2)}) collective-permute-start(bf16[256,2560]{1,0:T(8,128)(2,1)} %get-tuple-element.459.k_far.n_far), channel_id=1, source_target_pairs={{0,1},{1,0},{2,3},{3,2},{4,5},{5,4},{6,7},{7,6},{8,9},{9,8},{10,11... | collective-permute-start | bytes 3932168 | tf_op jit(solution)/shard_map/cond/branch_3_fun/cond/branch_1_fun/ppermute | solution.py:368
  52.3 29.1 %collective-permute-start.35 = (bf16[256,2048]{1,0:T(8,128)(2,1)}, bf16[256,2048]{1,0:T(8,128)(2,1)}, u32[]{:S(2)}, u32[]{:S(2)}) collective-permute-start(bf16[256,2048]{1,0:T(8,128)(2,1)} %get-tuple-element.488), channel_id=1, source_target_pairs={{0,32},{1,33},{2,34},{3,35},{4,36},{5,37},{6,38},{7,39},{8,40},{9,... | collective-permute-start | bytes 3145736 | tf_op jit(solution)/shard_map/cond/branch_3_fun/ppermute | solution.py:368
  62.5 4.5 %collective-permute-start.30 = (bf16[256,2048]{1,0:T(8,128)(2,1)}, bf16[256,2048]{1,0:T(8,128)(2,1)}, u32[]{:S(2)}, u32[]{:S(2)}) collective-permute-start(bf16[256,2048]{1,0:T(8,128)(2,1)} %get-tuple-element.472.n_far), channel_id=1, source_target_pairs={{0,1},{1,0},{2,3},{3,2},{4,5},{5,4},{6,7},{7,6},{8,9},{9,8},{10,11... | collective-permute-start | bytes 3145736 | tf_op jit(solution)/shard_map/cond/branch_3_fun/cond/branch_1_fun/ppermute | solution.py:368
  73.0 26.7 %collective-permute-start.34 = (bf16[256,2048]{1,0:T(8,128)(2,1)}, bf16[256,2048]{1,0:T(8,128)(2,1)S(1)}, u32[]{:S(2)}, u32[]{:S(2)}) collective-permute-start(bf16[256,2048]{1,0:T(8,128)(2,1)} %get-tuple-element.491), channel_id=1, source_target_pairs={{0,32},{1,33},{2,34},{3,35},{4,36},{5,37},{6,38},{7,39},{8,40},{9,... | collective-permute-start | bytes 3145736 | tf_op jit(solution)/shard_map/cond/branch_3_fun/ppermute | solution.py:368
  81.5 8.9 %collective-permute-start.36 = (bf16[256,512]{1,0:T(8,128)(2,1)}, bf16[256,512]{1,0:T(8,128)(2,1)S(1)}, u32[]{:S(2)}, u32[]{:S(2)}) collective-permute-start(bf16[256,512]{1,0:T(8,128)(2,1)} %project.17), channel_id=1, source_target_pairs={{0,2},{1,3},{2,0},{3,1},{4,6},{5,7},{6,4},{7,5},{8,10},{9,11},{10,... | collective-permute-start | bytes 786440 | tf_op jit(solution)/shard_map/cond/branch_3_fun/ppermute | solution.py:368
  90.4 0.7 copy-start.15
